TPU v7x, 32 devices: a whole 2x2x4 slice. The times are simulated.
32 devices in a mesh: seq: 2 (over core), shard: 16 (over z, y, x).
Axes of the slice: x: 2, y: 2, z: 4, core: 2. Of those that a mesh axis runs over, the one named last changes fastest.
Arguments:
- hidden_in: bfloat16 [16, 256, 2048], P('shard', 'seq'), may hold values from -6 to 6
- out_grad: bfloat16 [16, 256, 2048], P('shard', 'seq'), may hold values from -6 to 6
- segments: int32 [16, 256], P('shard'), may hold values from 0 to 2, as said below
- qkv_weight: float32 [2048, 4096], P(('seq', 'shard')), may hold values from -0.09375 to 0.09375
- out_weight: float32 [2048, 2048], P(('seq', 'shard')), may hold values from -0.75 to 0.75
- gateup_weight: float32 [2048, 16384], P(('seq', 'shard')), may hold values from -0.09375 to 0.09375
- down_weight: float32 [8192, 2048], P(('seq', 'shard')), may hold values from -0.0625 to 0.0625
- gain_weight: float32 [2, 2048], P(None, ('seq', 'shard'))
- qkv_first: float32 [2048, 4096], P(('seq', 'shard'))
- out_first: float32 [2048, 2048], P(('seq', 'shard'))
- gateup_first: float32 [2048, 16384], P(('seq', 'shard'))
- down_first: float32 [8192, 2048], P(('seq', 'shard'))
- gain_first: float32 [2, 2048], P(None, ('seq', 'shard'))
- qkv_second: float32 [2048, 4096], P(('seq', 'shard'))
- out_second: float32 [2048, 2048], P(('seq', 'shard'))
- gateup_second: float32 [2048, 16384], P(('seq', 'shard'))
- down_second: float32 [8192, 2048], P(('seq', 'shard'))
- gain_second: float32 [2, 2048], P(None, ('seq', 'shard'))
Outputs:
- output: bfloat16 [16, 256, 2048], P('shard', 'seq')
- input_grad: bfloat16 [16, 256, 2048], P('shard', 'seq')
- qkv_new: float32 [2048, 4096], P(('seq', 'shard'))
- out_new: float32 [2048, 2048], P(('seq', 'shard'))
- gateup_new: float32 [2048, 16384], P(('seq', 'shard'))
- down_new: float32 [8192, 2048], P(('seq', 'shard'))
- gain_new: float32 [2, 2048], P(None, ('seq', 'shard'))
- qkv_momentum: float32 [2048, 4096], P(('seq', 'shard'))
- out_momentum: float32 [2048, 2048], P(('seq', 'shard'))
- gateup_momentum: float32 [2048, 16384], P(('seq', 'shard'))
- down_momentum: float32 [8192, 2048], P(('seq', 'shard'))
- gain_momentum: float32 [2, 2048], P(None, ('seq', 'shard'))
- qkv_variance: float32 [2048, 4096], P(('seq', 'shard'))
- out_variance: float32 [2048, 2048], P(('seq', 'shard'))
- gateup_variance: float32 [2048, 16384], P(('seq', 'shard'))
- down_variance: float32 [8192, 2048], P(('seq', 'shard'))
- gain_variance: float32 [2, 2048], P(None, ('seq', 'shard'))
- qkv_copy: bfloat16 [2048, 4096], P(('seq', 'shard'))
- out_copy: bfloat16 [2048, 2048], P(('seq', 'shard'))
- gateup_copy: bfloat16 [2048, 16384], P(('seq', 'shard'))
- down_copy: bfloat16 [8192, 2048], P(('seq', 'shard'))
- gain_copy: bfloat16 [2, 2048], P(None, ('seq', 'shard'))
- trust_norms: float32 [2, 6], replicated
Inputs may be any that keep to these rules, and one draw needn't show every extreme that they name: `segments`: each row is one prompt group: ids never fall along the row; id 0 marks the prompt, which holds more than half of the row; ids 1 to 2 mark the continuations in order, each with one token or more.
All inputs are finite; a program needn't handle non-finite values.
Results may differ from a plain program's by a relative error of at most 0.015.
The roundings to bfloat16 on the way count: a program that leaves them out, or rounds other values in their place, can miss the bound.
Values may be sent and summed in bfloat16 or wider, within the bound.
No kernel may reach another device: no remote copies, remote signals or barrier semaphores. Data moves between devices by JAX's collectives and lax.ppermute only.
A program may use at most 960 MiB of HBM per device.

v0:
```python
import jax
import jax.numpy as jnp
import numpy as np
from jax import lax
from jax.experimental import pallas as pl
from jax.experimental.pallas import tpu as pltpu
from jax.sharding import PartitionSpec as P

HQ = 16
KVH = 8
HD = 128
FF = 8192
NCONT = 2
STEP = 10
TP = 4


NORM_EPS = 1e-05
THETA = 1000000.0
BETA1 = 0.9
BETA2 = 0.999
ADAM_EPS = 1e-06
DECAY = 0.01
RATE = 0.5
MASKED = -1e30
GROUP = HQ // KVH
HEAD_COLS = (GROUP + 2) * HD
BF = jnp.bfloat16
F32 = jnp.float32


def dot(left, right):
    return jnp.dot(left, right, preferred_element_type=F32)


def dot_rows(left, right):
    return lax.dot_general(left, right, (((0,), (0,)), ((), ())), preferred_element_type=F32)


def dot_last(left, right):
    return lax.dot_general(left, right, (((1,), (1,)), ((), ())), preferred_element_type=F32)


def after(values, *others):
    return lax.optimization_barrier((values, *others))[0]


RECENT = []


def permute(values, axis, pairs):
    RECENT.append(lax.ppermute(values, axis, pairs))
    return RECENT[-1]


def recent():
    arrivals = tuple(RECENT)
    RECENT.clear()
    return arrivals


def shard_size():
    return lax.axis_size("shard")


def place_size():
    return shard_size() // TP


def shard_bits(count):
    return count.bit_length() - 1


def place_index():
    return lax.axis_index("shard") % place_size()


def column_index():
    return lax.axis_index("shard") // place_size()


def corner_index():
    return lax.axis_index("shard") % TP


def line_index():
    return lax.axis_index("shard") // TP


def line_place(line):
    middles = place_size() // TP
    return line % middles * TP + line // middles


def rotate(values, steps):
    count, places = shard_size(), place_size()
    pairs = [
        (entry, ((entry // places - steps) % TP) * places + entry % places)
        for entry in range(count)
    ]
    return permute(values, "shard", pairs)


def hop(values, change):
    return permute(values, "shard", [(i, i ^ change) for i in range(shard_size())])


def swap_roles(values):
    count, places = shard_size(), place_size()

    def partner(entry):
        column, middle, corner = entry // places, entry % places // TP, entry % TP
        return (corner * (places // TP) + middle) * TP + column

    return permute(values, "shard", [(i, partner(i)) for i in range(count)])


def flip(values):
    return permute(values, "seq", [(0, 1), (1, 0)])


def butterfly(values):
    for bit in reversed(range(shard_bits(shard_size()))):
        values = values + hop(values, 1 << bit)
    return values + flip(values)


def from_column(values, step):
    return rotate(values, step) if step else values


def to_column(values, step):
    return rotate(values, -step) if step else values


def from_corner(values, step):
    return hop(values, step) if step else values


def ride(load, extra):
    columns = load.shape[1]
    count = -(-extra.size // (16 * columns)) * 16 * columns
    extra = jnp.pad(extra.reshape(-1).astype(BF), (0, count - extra.size))
    return jnp.concatenate([load, extra.reshape(-1, columns)], axis=0)


def alight(load, rows, shape):
    size = 1
    for entry in shape:
        size *= entry
    return load[:rows], load[rows:].reshape(-1)[:size].reshape(shape)


def both_halves(mine):
    mine = jnp.concatenate(mine, axis=0)
    return jnp.concatenate([mine, flip(mine)], axis=0)


def meet_halves(mine, other):
    return jnp.split(mine + flip(other).astype(F32), TP)


def gather_bits(own, low_bit, bits):
    blocks = {0: own}
    for bit in range(bits):
        for entry in list(blocks):
            blocks[entry | (1 << bit)] = hop(blocks[entry], 1 << (low_bit + bit))
    return [blocks[entry] for entry in range(1 << bits)]


def scatter_bits(blocks, low_bit, bits):
    sums = {entry: block.astype(F32) for entry, block in enumerate(blocks)}
    for bit in reversed(range(bits)):
        for entry in range(1 << bit):
            came = hop(sums.pop(entry | (1 << bit)).astype(BF), 1 << (low_bit + bit))
            sums[entry] = sums[entry] + came.astype(F32)
    return sums[0]


def gather_places(own):
    places = place_size()
    groups = [[column * places + place for place in range(places)] for column in range(TP)]
    return lax.all_gather(own, "shard", axis_index_groups=groups)


def scatter_places(block_of, hold=(), finish=True):
    blocks = [block_of(place_index() ^ entry) for entry in range(place_size())]
    if place_size() != TP:
        total = scatter_bits(blocks, 0, shard_bits(place_size()))
        return total if finish else [total]
    blocks[3] = after(blocks[3], *hold)
    parts = [from_corner(blocks[j], j) for j in range(TP)]
    return sum(part.astype(F32) for part in parts) if finish else parts


def gather_lines(own):
    if place_size() == TP:
        return [((column_index() + k) % TP, from_column(own, k)) for k in range(TP)]
    blocks = gather_bits(own, 2, shard_bits(place_size()))
    return [(line_index() ^ entry, block) for entry, block in enumerate(blocks)]


def scatter_lines(block_of):
    if place_size() == TP:
        total = None
        for step in range(TP):
            came = to_column(block_of((column_index() + step) % TP), step).astype(F32)
            total = came if total is None else total + came
        return total
    return scatter_bits(
        [block_of(line_index() ^ entry) for entry in range(place_size())],
        2,
        shard_bits(place_size()),
    )


def lay(blocks, axis):
    shape = blocks[0][1].shape
    full = jnp.zeros(shape[:axis] + (len(blocks),) + shape[axis:], blocks[0][1].dtype)
    for index, block in blocks:
        starts = [0] * full.ndim
        starts[axis] = index
        full = lax.dynamic_update_slice(full, jnp.expand_dims(block, axis), starts)
    return full


def pick(values, index, axis):
    return lax.dynamic_index_in_dim(values, index, axis, keepdims=False)


def ordered_pair(mine, other):
    first = lax.axis_index("seq") == 0
    return jnp.stack([jnp.where(first, mine, other), jnp.where(first, other, mine)])


def turn_columns(blocks):
    twice = jnp.stack(blocks + blocks)
    return lax.dynamic_slice_in_dim(twice, (TP - column_index()) % TP, TP, 0)


def turn_corners(blocks):
    corner = corner_index()
    for bit in (1, 2):
        odd = corner // bit % 2 == 1
        blocks = [jnp.where(odd, blocks[j ^ bit], blocks[j]) for j in range(TP)]
    return jnp.stack(blocks)


def columns_of(source, starts, size):
    return jnp.concatenate(
        [lax.dynamic_slice_in_dim(source, start, size, 1) for start in starts], axis=1
    )


def pair_qkv(weight):
    seq = lax.axis_index("seq")
    half = TP * HEAD_COLS
    mine = columns_of(weight, [seq * half], half)
    other = flip(columns_of(weight, [(1 - seq) * half], half))
    return ordered_pair(mine, other).reshape(-1, half)


def qkv_piece(pair, step):
    return columns_of(pair, [(corner_index() ^ step) * HEAD_COLS], HEAD_COLS)


def unspread_qkv(total, rows, rider):
    corner, seq = corner_index(), lax.axis_index("seq")
    count = rider.shape[-1]
    loads = [
        ride(pick(total, corner ^ j, 1).reshape(-1, HEAD_COLS), pick(rider, corner ^ j, 2))
        for j in range(TP)
    ]
    loads = [alight(from_corner(loads[j], j), 2 * rows, (2, 2, count)) for j in range(TP)]
    laid = turn_corners([load.reshape(2, rows, HEAD_COLS) for load, _ in loads])
    rider = sum(extra.astype(F32) for _, extra in loads)
    load = ride(pick(laid, 1 - seq, 1).reshape(-1, HEAD_COLS), pick(rider, 1 - seq, 1))
    other, extra = alight(flip(load), TP * rows, (2, count))
    rider = pick(rider, seq, 1) + extra.astype(F32)
    both = ordered_pair(pick(laid, seq, 1), other.reshape(TP, rows, HEAD_COLS))
    return jnp.concatenate([both[s, q] for s in range(2) for q in range(TP)], axis=1), rider


def pair_gateup(weight):
    seq, span = lax.axis_index("seq"), FF // 2
    mine = columns_of(weight, [seq * span, FF + seq * span], span)
    other = flip(columns_of(weight, [(1 - seq) * span, FF + (1 - seq) * span], span))
    return ordered_pair(mine, other).reshape(-1, FF)


def spread_gateup(pair, rider):
    column, span = column_index(), FF // (2 * TP)
    loads = []
    for k in range(TP):
        start = (column - k) % TP * span
        piece = columns_of(pair, [start, FF // 2 + start], span)
        loads.append(from_column(ride(piece, rider), k))
    loads = [alight(load, pair.shape[0], rider.shape) for load in loads]
    return jnp.concatenate([load for load, _ in loads], axis=0), [extra for _, extra in loads]


def collect_lines(block):
    shape = block.shape
    blocks = [
        (index, came.reshape(shape)) for index, came in gather_lines(block.reshape(-1, shape[-1]))
    ]
    return lay(blocks, 1).reshape(-1, shape[-1])


def order_places(came):
    places, columns = place_size(), came.shape[-1]
    came = came.reshape(places, TP, 2, -1, columns)
    full = jnp.zeros((2, TP, places, came.shape[3], columns), came.dtype)
    for k in range(TP):
        part = jnp.swapaxes(came[:, k], 0, 1)[:, None]
        full = lax.dynamic_update_slice(full, part, (0, (column_index() + k) % TP, 0, 0, 0))
    return full.reshape(-1, columns)


def place_parts(values, rows, hold=()):
    span = values.shape[1]
    view = values.reshape(2, TP, place_size(), rows, span)
    return scatter_places(lambda place: pick(view, place, 2).reshape(-1, span), hold, False)


def place_total(parts, rows):
    total = sum(part.astype(F32) for part in parts)
    return total.astype(BF).reshape(2, TP, rows, -1)


def column_piece(total, step):
    return pick(total, (column_index() - step) % TP, 1)


def lay_columns(pieces):
    laid = turn_columns(pieces)
    seq = lax.axis_index("seq")
    return ordered_pair(pick(laid, seq, 1), flip(pick(laid, 1 - seq, 1)))


def norm_scale(values):
    return lax.rsqrt(jnp.mean(values * values, axis=-1, keepdims=True) + NORM_EPS)


def positions_of(seg_row):
    labels = jnp.arange(NCONT + 1, dtype=jnp.int32)
    member = (seg_row[:, None] == labels[None, :]).astype(jnp.int32)
    counts = jnp.sum(member, axis=0)
    starts = jnp.cumsum(counts) - counts
    own_start = jnp.sum(member * starts[None, :], axis=1)
    places = jnp.arange(seg_row.shape[0], dtype=jnp.int32)
    return places - own_start + jnp.where(seg_row > 0, counts[0], 0)


def rotary(positions):
    half_size = HD // 2
    frequency = THETA ** (-(jnp.arange(half_size, dtype=F32) * (2.0 / HD)))
    angles = positions.astype(F32)[:, None] * frequency[None, :]
    angles = jnp.concatenate([angles, angles], axis=-1)
    return (jnp.cos(angles), jnp.sin(angles))


def norm_back(d_normed, inputs_f, factor_rows, gain_row):
    weighted = d_normed * gain_row
    d_inputs = factor_rows * weighted - inputs_f * factor_rows**3 * jnp.mean(
        weighted * inputs_f, axis=-1, keepdims=True
    )
    d_gain = jnp.sum(d_normed * inputs_f * factor_rows, axis=0)
    return (d_inputs, d_gain)


def lamb_step(master, gradient, old_one, old_two, decay_rate):
    new_one = BETA1 * old_one + (1.0 - BETA1) * gradient
    new_two = BETA2 * old_two + (1.0 - BETA2) * gradient * gradient
    update = (
        new_one / (1.0 - BETA1**STEP) / (jnp.sqrt(new_two / (1.0 - BETA2**STEP)) + ADAM_EPS)
        + decay_rate * master
    )
    return new_one, new_two, update


SMALL = pl.CostEstimate(flops=10**9, bytes_accessed=1, transcendentals=0)
MIB = 1 << 20


def params(mebibytes):
    return pltpu.CompilerParams(vmem_limit_bytes=mebibytes * MIB)


def whole(shape):
    return pl.BlockSpec(shape, lambda step: (0,) * len(shape), pipeline_mode=pl.Buffered(1))


def at_group(shape, axis):
    return pl.BlockSpec(shape, lambda step: tuple(step if d == axis else 0 for d in range(len(shape))))


def half_sign():
    lane = lax.broadcasted_iota(jnp.int32, (1, HD), 1)
    return jnp.where(lane < HD // 2, -1.0, 1.0)


def scores_of(query, key_rows, allowed):
    return jnp.where(allowed, dot_last(query, key_rows) * HD ** (-0.5), MASKED)


def allowed_of(place_col, place_row, id_col, id_row):
    return (place_row <= place_col) & ((id_row == 0) | (id_row == id_col))


def attend_kernel(
    x_ref, gain_ref, qkv_ref, cos_ref, sin_ref, place_col, place_row, id_col, id_row,
    turned_ref, lse_ref, attended_ref,
):
    tokens = cos_ref.shape[1]
    x = x_ref[...].reshape(tokens, -1).astype(F32)
    normed = (x * norm_scale(x) * gain_ref[...]).astype(BF)
    projected = dot(normed, qkv_ref[...])
    cosine, sine = cos_ref[0], sin_ref[0] * half_sign()
    turned = []
    for head in range(GROUP + 2):
        values = projected[:, head * HD : (head + 1) * HD]
        if head <= GROUP:
            values = values * cosine + pltpu.roll(values, HD // 2, 1) * sine
        turned.append(values.astype(BF))
        turned_ref[0, :, head * HD : (head + 1) * HD] = turned[head]
    allowed = allowed_of(place_col[...], place_row[...], id_col[0], id_row[0])
    for head in range(GROUP):
        scores = scores_of(turned[head], turned[GROUP], allowed)
        row_max = jnp.max(scores, axis=-1, keepdims=True)
        exponent = jnp.exp(scores - row_max)
        row_total = jnp.sum(exponent, axis=-1, keepdims=True)
        lse_ref[0, head] = row_max + jnp.log(row_total)
        rows_out = dot((exponent / row_total).astype(BF), turned[GROUP + 1]).astype(BF)
        attended_ref[:, 0, :, head * HD : (head + 1) * HD] = rows_out.reshape(2, tokens // 2, HD)


def attend(x_all, gain, qkv_matrix, cosine, sine, marks):
    _, groups, half_tok, width = x_all.shape
    tokens = 2 * half_tok
    by_half = lambda columns: at_group((2, 1, half_tok, columns), 1)
    return pl.pallas_call(
        attend_kernel,
        grid=(groups,),
        in_specs=[
            by_half(width),
            whole((1, width)),
            whole((width, HEAD_COLS)),
            at_group((1, tokens, HD), 0),
            at_group((1, tokens, HD), 0),
            whole((tokens, 1)),
            whole((1, tokens)),
            at_group((1, tokens, 1), 0),
            at_group((1, 1, tokens), 0),
        ],
        out_specs=[
            at_group((1, tokens, HEAD_COLS), 0),
            at_group((1, GROUP, tokens, 1), 0),
            by_half(GROUP * HD),
        ],
        out_shape=[
            jax.ShapeDtypeStruct((groups, tokens, HEAD_COLS), BF),
            jax.ShapeDtypeStruct((groups, GROUP, tokens, 1), F32),
            jax.ShapeDtypeStruct((2, groups, half_tok, GROUP * HD), BF),
        ],
        compiler_params=params(32),
        cost_estimate=SMALL,
    )(x_all, gain, qkv_matrix, cosine, sine, *marks)


def attend_back_kernel(
    branch_ref, out_ref, qkv_ref, x_ref, gain_ref, attended_ref, turned_ref, lse_ref, cos_ref, sin_ref,
    place_col, place_row, id_col, id_row,
    mine_ref, other_ref, grad_qkv_ref, grad_out_ref, grad_gain_ref, qkv_sum, out_sum,
):
    tokens = cos_ref.shape[1]
    factor = HD ** (-0.5)
    first = pl.program_id(0) == 0
    last = pl.program_id(0) == pl.num_programs(0) - 1
    branch = branch_ref[...].reshape(tokens, -1)
    d_attended = dot_last(branch, out_ref[...]).astype(BF)
    turned = [turned_ref[0, :, head * HD : (head + 1) * HD] for head in range(GROUP + 2)]
    key_rows, value_rows = turned[GROUP], turned[GROUP + 1]
    allowed = allowed_of(place_col[...], place_row[...], id_col[0], id_row[0])
    cosine, sine, sign = cos_ref[0], sin_ref[0], half_sign()

    def unrope(values):
        values = values.astype(BF).astype(F32)
        return (values * cosine - sign * pltpu.roll(values * sine, HD // 2, 1)).astype(BF)

    d_keys = d_values = None
    columns = []
    for head in range(GROUP):
        d_rows = d_attended[:, head * HD : (head + 1) * HD]
        probs = jnp.exp(scores_of(turned[head], key_rows, allowed) - lse_ref[0, head])
        d_probs = dot_last(d_rows, value_rows)
        row_sum = jnp.sum(probs * d_probs, axis=-1, keepdims=True)
        d_scores = (probs * (d_probs - row_sum)).astype(BF)
        columns.append(unrope(dot(d_scores, key_rows) * factor))
        key_part = dot_rows(d_scores, turned[head]) * factor
        value_part = dot_rows(probs.astype(BF), d_rows)
        d_keys = key_part if d_keys is None else d_keys + key_part
        d_values = value_part if d_values is None else d_values + value_part
    columns.append(unrope(d_keys))
    columns.append(d_values.astype(BF))
    projected = jnp.concatenate(columns, axis=1)
    d_normed = dot_last(projected, qkv_ref[...])
    mine_ref[0] = d_normed[: tokens // 2]
    other_ref[0] = d_normed[tokens // 2 :].astype(BF)

    @pl.when(first)
    def _():
        qkv_sum[...] = jnp.zeros_like(qkv_sum)
        out_sum[...] = jnp.zeros_like(out_sum)
        grad_gain_ref[...] = jnp.zeros_like(grad_gain_ref)

    x = x_ref[...].reshape(tokens, -1).astype(F32)
    scaled = x * norm_scale(x)
    grad_gain_ref[...] += jnp.sum(d_normed * scaled, axis=0, keepdims=True)
    qkv_sum[...] += dot_rows((scaled * gain_ref[...]).astype(BF), projected)
    out_sum[...] += dot_rows(attended_ref[...].reshape(tokens, -1), branch)

    @pl.when(last)
    def _():
        grad_qkv_ref[...] = qkv_sum[...].astype(BF)
        grad_out_ref[...] = out_sum[...].astype(BF)


def attend_back(d_branch, out_matrix, qkv_matrix, x_all, gain, attended, turned, lse, cosine, sine, marks):
    _, groups, half_tok, width = d_branch.shape
    tokens = 2 * half_tok
    return pl.pallas_call(
        attend_back_kernel,
        grid=(groups,),
        in_specs=[
            at_group((2, 1, half_tok, width), 1),
            whole((GROUP * HD, width)),
            whole((width, HEAD_COLS)),
            at_group((2, 1, half_tok, width), 1),
            whole((1, width)),
            at_group((2, 1, half_tok, GROUP * HD), 1),
            at_group((1, tokens, HEAD_COLS), 0),
            at_group((1, GROUP, tokens, 1), 0),
            at_group((1, tokens, HD), 0),
            at_group((1, tokens, HD), 0),
            whole((tokens, 1)),
            whole((1, tokens)),
            at_group((1, tokens, 1), 0),
            at_group((1, 1, tokens), 0),
        ],
        out_specs=[
            at_group((1, half_tok, width), 0),
            at_group((1, half_tok, width), 0),
            whole((width, HEAD_COLS)),
            whole((GROUP * HD, width)),
            whole((1, width)),
        ],
        out_shape=[
            jax.ShapeDtypeStruct((groups, half_tok, width), F32),
            jax.ShapeDtypeStruct((groups, half_tok, width), BF),
            jax.ShapeDtypeStruct((width, HEAD_COLS), BF),
            jax.ShapeDtypeStruct((GROUP * HD, width), BF),
            jax.ShapeDtypeStruct((1, width), F32),
        ],
        scratch_shapes=[pltpu.VMEM((width, HEAD_COLS), F32), pltpu.VMEM((GROUP * HD, width), F32)],
        compiler_params=params(48),
        cost_estimate=SMALL,
    )(d_branch, out_matrix, qkv_matrix, x_all, gain, attended, turned, lse, cosine, sine, *marks)


def half_specs(rows, columns, steps):
    first = pl.BlockSpec((rows, columns), lambda step: (jnp.minimum(step, steps // 2 - 1), 0))
    second = pl.BlockSpec((rows, columns), lambda step: (jnp.maximum(step - steps // 2, 0), 0))
    shapes = [
        jax.ShapeDtypeStruct((rows * steps // 2, columns), F32),
        jax.ShapeDtypeStruct((rows * steps // 2, columns), BF),
    ]
    return [first, second], shapes


def store_halves(values, mine_ref, other_ref):
    step, half = pl.program_id(0), pl.num_programs(0) // 2

    @pl.when(step < half)
    def _():
        mine_ref[...] = values

    @pl.when(step >= half)
    def _():
        other_ref[...] = values.astype(BF)


def partial_kernel(left_ref, right_ref, mine_ref, other_ref):
    store_halves(dot(left_ref[...], right_ref[...]), mine_ref, other_ref)


def partial_product(left, right):
    tokens, depth = left.shape
    rows, steps = tokens // 4, 4
    specs, shapes = half_specs(rows, right.shape[1], steps)
    return pl.pallas_call(
        partial_kernel,
        grid=(steps,),
        in_specs=[at_group((rows, depth), 0), whole(right.shape)],
        out_specs=specs,
        out_shape=shapes,
        compiler_params=params(32),
        cost_estimate=SMALL,
    )(left, right)


def forward_back_kernel(
    normed_ref, og_ref, matrix_ref, down_ref,
    activated_ref, d_first_ref, d_second_ref, mine_ref, other_ref,
):
    width = matrix_ref.shape[1] // 4
    normed, og = normed_ref[...], og_ref[...]
    total = None
    for half, d_ref in enumerate((d_first_ref, d_second_ref)):
        gate_matrix = matrix_ref[:, half * width : (half + 1) * width]
        up_matrix = matrix_ref[:, (2 + half) * width : (3 + half) * width]
        gate, up = dot(normed, gate_matrix), dot(normed, up_matrix)
        d_act = dot_last(og, down_ref[half * width : (half + 1) * width])
        sigmoid = jax.nn.sigmoid(gate)
        silu = gate * sigmoid
        activated_ref[:, half * width : (half + 1) * width] = (silu * up).astype(BF)
        d_ref[:, :width] = (d_act * up * (sigmoid * (1.0 + gate * (1.0 - sigmoid)))).astype(BF)
        d_ref[:, width:] = (d_act * silu).astype(BF)
        back = dot_last(d_ref[:, :width], gate_matrix) + dot_last(d_ref[:, width:], up_matrix)
        total = back if total is None else total + back
    store_halves(total, mine_ref, other_ref)


def forward_back(normed2, og_all, gateup_matrix, down_matrix):
    tokens, width = normed2.shape
    unit = down_matrix.shape[0]
    rows, steps = tokens // 4, 4
    specs, shapes = half_specs(rows, width, steps)
    return pl.pallas_call(
        forward_back_kernel,
        grid=(steps,),
        in_specs=[
            at_group((rows, width), 0),
            at_group((rows, width), 0),
            whole((width, 2 * unit)),
            whole((unit, width)),
        ],
        out_specs=[at_group((rows, unit), 0)] * 3 + specs,
        out_shape=[jax.ShapeDtypeStruct((tokens, unit), BF)] * 3 + shapes,
        compiler_params=params(48),
        cost_estimate=SMALL,
    )(normed2, og_all, gateup_matrix, down_matrix)


def gradient_kernel(left_ref, right_ref, out_ref):
    out_ref[...] = dot_rows(left_ref[...], right_ref[...]).astype(BF)


def gradient(left, right):
    tokens, rows = left.shape
    block = min(rows, 256)
    return pl.pallas_call(
        gradient_kernel,
        grid=(rows // block,),
        in_specs=[at_group((tokens, block), 1), whole(right.shape)],
        out_specs=at_group((block, right.shape[1]), 0),
        out_shape=jax.ShapeDtypeStruct((rows, right.shape[1]), BF),
        compiler_params=params(32),
        cost_estimate=SMALL,
    )(left, right)


def lamb_kernel(
    master_ref, one_ref, two_ref, first_ref, second_ref, new_one_ref, new_two_ref, update_ref, sums_ref
):
    gradient = jnp.concatenate([first_ref[0, 0], second_ref[0, 0]], axis=1).astype(F32)
    master = master_ref[...]
    new_one, new_two, update = lamb_step(master, gradient, one_ref[...], two_ref[...], DECAY)
    new_one_ref[...], new_two_ref[...], update_ref[...] = new_one, new_two, update

    @pl.when(pl.program_id(0) == 0)
    def _():
        sums_ref[...] = jnp.zeros_like(sums_ref)

    sums_ref[0:1] += jnp.sum(master * master, axis=0, keepdims=True)
    sums_ref[1:2] += jnp.sum(update * update, axis=0, keepdims=True)


def lamb_gateup(master, old_one, old_two, halves):
    rows, columns = master.shape
    span = columns // (4 * TP)
    state = pl.BlockSpec((rows, span), lambda step: (0, step))
    piece = pl.BlockSpec(
        (1, 1, rows, span // 2), lambda step: (step // TP % 2, step % TP, 0, step // (2 * TP))
    )
    shape = jax.ShapeDtypeStruct(master.shape, F32)
    return pl.pallas_call(
        lamb_kernel,
        grid=(4 * TP,),
        in_specs=[state] * 3 + [piece] * 2,
        out_specs=[state] * 3 + [whole((2, span))],
        out_shape=[shape] * 3 + [jax.ShapeDtypeStruct((2, span), F32)],
        compiler_params=params(32),
        cost_estimate=SMALL,
    )(master, old_one, old_two, *halves)


def shards(
    hidden_in,
    out_grad,
    segments,
    qkv_weight,
    out_weight,
    gateup_weight,
    down_weight,
    gain_weight,
    qkv_first,
    out_first,
    gateup_first,
    down_first,
    gain_first,
    qkv_second,
    out_second,
    gateup_second,
    down_second,
    gain_second,
):
    seq = lax.axis_index("seq")
    rows = qkv_weight.shape[0]
    tok_local = hidden_in.shape[1]
    group_tok = tok_local * lax.axis_size("seq")
    span = TP * tok_local
    owner = seq * shard_size() + lax.axis_index("shard")


    x_own, og_own = hidden_in[0], out_grad[0]
    x_local = x_own.astype(F32)
    recent()

    gain_cols, width = gain_weight.shape[1], x_own.shape[1]
    packed = place_size() == TP
    shard = lax.axis_index("shard")
    gain_low = gain_weight.astype(BF)
    info = jnp.concatenate([gain_low.reshape(-1), segments.reshape(-1).astype(BF)])
    og_mine = [og_own, from_column(og_own, 1), None, from_column(og_own, 3)]
    came = recent()
    qkv_pair = pair_qkv(qkv_weight.astype(BF))
    pair = pair_gateup(gateup_weight.astype(BF))
    pairs_came = recent()
    loads = [
        jnp.concatenate([x_own, qkv_piece(qkv_pair, j).reshape(tok_local, -1)], axis=1)
        for j in range(TP)
    ]
    loads = [ride(load, info) for load in loads]
    loads[3] = after(loads[3], *came[:1])
    loads = [from_corner(loads[j], j) for j in range(TP)]
    loads = [alight(load, tok_local, info.shape) for load in loads]
    x_mine = [load[:, :width] for load, _ in loads]
    infos = jnp.stack([extra for _, extra in loads])
    qkv_block = turn_corners([load[:, width:].reshape(-1, HEAD_COLS) for load, _ in loads])
    qkv_block = jnp.swapaxes(qkv_block.reshape(TP, 2, rows, HEAD_COLS), 0, 1)
    slot = (*came, *pairs_came, *recent())
    ids = [infos[j, 2 * gain_cols :].astype(jnp.int32) for j in range(TP)]

    down_matrix = gather_places(after(down_weight.astype(BF), *slot)).reshape(-1, width)
    gateup_block, infos = spread_gateup(after(pair, *slot), infos)
    infos = jnp.stack(infos)
    out_block = swap_roles(after(out_weight.astype(BF), *slot))
    slot = recent()

    qkv_matrix = collect_lines(after(qkv_block, *slot))
    came = recent()
    gateup_came = gather_places(after(gateup_block, down_matrix))
    gateup_matrix = order_places(gateup_came)
    x_half = jnp.concatenate([after(x_mine[0], *slot, down_matrix), *x_mine[1:]], axis=0)
    x_other, infos_other = alight(flip(ride(x_half, infos)), span, infos.shape)
    x_all = jnp.concatenate([x_half, x_other], axis=0).reshape(2, TP, tok_local, width)
    if packed:
        gains = ordered_pair(infos, infos_other)[..., : 2 * gain_cols]
        gains = turn_columns([turn_corners([gains[:, k, j] for j in range(TP)]) for k in range(TP)])
        gains = jnp.transpose(gains.reshape(TP, TP, 2, 2, gain_cols), (3, 2, 0, 1, 4)).reshape(2, width)
    else:
        gains = jnp.zeros((2, width), BF)
        gains = butterfly(lax.dynamic_update_slice(gains, gain_low, (0, owner * gain_cols)))
    gains = gains.astype(F32)
    slot = (*came, *recent(), x_all, gains)

    def local_order(values):
        return jnp.where(seq == 0, values, jnp.roll(values, -tok_local, axis=-1))

    positions = jnp.stack([local_order(positions_of(entry)) for entry in ids])
    ids = jnp.stack([local_order(entry) for entry in ids])
    places = local_order(jnp.arange(group_tok, dtype=jnp.int32))
    marks = (places[:, None], places[None, :], ids[:, :, None], ids[:, None, :])
    cosine, sine = rotary(positions.reshape(-1))
    cosine, sine = cosine.reshape(TP, group_tok, HD), sine.reshape(TP, group_tok, HD)

    out_matrix = lay(
        [(line_place(line), block) for line, block in gather_lines(after(out_block, *slot))], 0
    ).reshape(GROUP * HD, -1)
    came = recent()
    og_mine[2] = from_column(after(og_own, *slot), 2)
    recent()
    turned, lse, attended = attend(x_all, gains[:1], qkv_matrix, cosine, sine, marks)
    attended = attended.reshape(-1, GROUP * HD)
    slot = (*came, attended)

    met = meet_halves(*partial_product(after(attended, *slot, gateup_came), out_matrix))
    middle = x_local + met[0]
    for j in range(1, TP):
        middle = middle + from_corner(met[j].astype(BF), j).astype(F32)
    factor_two = norm_scale(middle)
    slot = recent()

    og_all = both_halves([after(entry, *slot) for entry in og_mine])
    recent()

    normed2_own = after((middle * factor_two * gains[1]).astype(BF), *slot, og_mine[2])
    normed2 = [from_column(normed2_own, k) for k in range(TP)]
    normed2 = both_halves([after(normed2[0], gateup_matrix, *recent()), *normed2[1:]])
    slot = recent()

    activated, d_gate_up_0, d_gate_up_1, d_mine, d_other = forward_back(
        after(normed2, *slot), og_all, gateup_matrix, down_matrix
    )

    d_met = meet_halves(d_mine, d_other)
    slot = recent()
    sends = [entry.astype(BF) for entry in d_met[1:]]
    grad_half_0 = gradient(after(normed2, d_other), d_gate_up_0)
    total_0 = place_total(place_parts(after(grad_half_0, *slot), rows), rows)
    out_mine, out_other = partial_product(after(activated, *slot, grad_half_0), down_matrix)
    grad_half_1 = gradient(after(normed2, *slot, grad_half_0), d_gate_up_1)
    d_normed2 = d_met[0]
    for k in range(1, TP):
        came = after(to_column(sends[k - 1], k), out_other, grad_half_1)
        d_normed2 = d_normed2 + came.astype(F32)
    d_mid_part, d_gain_two = norm_back(d_normed2, middle, factor_two, gains[1])
    d_middle = og_own.astype(F32) + d_mid_part
    slot = recent()

    d_branch_own = after(d_middle.astype(BF), *slot)
    d_branch_mine = [from_corner(d_branch_own, j) for j in range(TP)]
    came = recent()
    held = after(total_0, *slot, d_branch_own)
    pieces = [column_piece(held, k) for k in range(TP)]
    pieces[3] = after(pieces[3], *came)
    laid_0 = lay_columns([from_column(pieces[k], k) for k in range(TP)])
    out_met = meet_halves(out_mine, after(out_other, *slot))
    slot = (*came, *recent()[:3])

    sends = [after(entry.astype(BF), *slot) for entry in out_met]
    result = middle + out_met[0]
    for k in range(1, TP):
        result = result + to_column(sends[k], k).astype(F32)
    output = result.astype(BF)[None]
    out_came = recent()
    parts_1 = place_parts(after(grad_half_1, *slot), rows, out_came[:1])
    out_came = (*out_came, *recent())
    d_branch = both_halves([after(entry, *slot) for entry in d_branch_mine])
    in_mine, in_other, grad_qkv, grad_out, d_gain_one = attend_back(
        d_branch.reshape(2, TP, tok_local, width),
        out_matrix,
        qkv_matrix,
        x_all,
        gains[:1],
        attended.reshape(2, TP, tok_local, GROUP * HD),
        turned,
        lse,
        cosine,
        sine,
        marks,
    )
    grad_down = gradient(after(activated, *slot), og_all)
    in_other = after(in_other.reshape(-1, width), *out_came, grad_down)
    in_met = meet_halves(in_mine.reshape(-1, width), in_other)
    slot = (*recent(), *out_came)

    d_normed = in_met[0]
    for j in range(1, TP):
        d_normed = d_normed + from_corner(after(in_met[j].astype(BF), *slot), j).astype(F32)
    came = recent()
    d_gains = jnp.concatenate([d_gain_one, d_gain_two[None]], axis=0)
    qkv_view = after(grad_qkv, *slot).reshape(2, place_size(), TP, rows, HEAD_COLS)
    out_view = after(grad_out, *slot).reshape(place_size(), -1, width)
    if packed:
        rider = d_gains.reshape(2, 2, TP, TP, gain_cols)
        qkv_rows, loads = 2 * TP * rows, []
        for k in range(TP):
            line = (column_index() + k) % TP
            load = [pick(qkv_view, line, 1), pick(out_view, line, 0)]
            load = jnp.concatenate([entry.reshape(-1, HEAD_COLS) for entry in load], axis=0)
            loads.append(ride(load, pick(rider, line, 2)))
        sent_rows = qkv_rows + out_view.shape[1] * width // HEAD_COLS
        loads[3] = after(loads[3], *came)
        loads = [to_column(loads[k], k) for k in range(TP)]
        loads = [alight(entry, sent_rows, (2, 2, TP, gain_cols)) for entry in loads]
        rider = sum(extra.astype(F32) for _, extra in loads)
        qkv_total = sum(load[:qkv_rows].astype(F32) for load, _ in loads)
        grad_out = sum(load[qkv_rows:].astype(F32) for load, _ in loads).reshape(-1, width)
    else:
        qkv_total = scatter_lines(lambda line: pick(qkv_view, line, 1).reshape(-1, HEAD_COLS))
        grad_out = scatter_lines(lambda line: pick(out_view, line_place(line), 0))
        rider = jnp.zeros((2, 2, TP, gain_cols), F32)
    slot = recent()
    down_view = after(grad_down, *came).reshape(place_size(), -1, width)
    grad_down = scatter_places(lambda place: pick(down_view, place, 0), slot[:1])
    slot = (*came, *slot, *recent()[:2])
    factor_one = norm_scale(x_local)
    d_in_part = norm_back(d_normed, x_local, factor_one, gains[0])[0]
    input_grad = (d_middle + d_in_part).astype(BF)[None]

    held = after(place_total([after(part, *came) for part in parts_1], rows), *slot)
    laid_1 = lay_columns([from_column(column_piece(held, k), k) for k in range(TP)])
    qkv_total = after(qkv_total.astype(BF), *slot).reshape(2, TP, rows, HEAD_COLS)
    grad_qkv, grad_gain = unspread_qkv(qkv_total, rows, rider)
    grad_qkv = grad_qkv.astype(F32)
    grad_out = swap_roles(after(grad_out.astype(BF), *slot)).astype(F32)
    if not packed:
        grad_gain = lax.dynamic_slice_in_dim(butterfly(d_gains), owner * gain_cols, gain_cols, 1)

    masters = (qkv_weight, out_weight, gateup_weight, down_weight, gain_weight)
    gateup_one, gateup_two, gateup_update, gateup_sums = lamb_gateup(
        gateup_weight, gateup_first, gateup_second, [laid_0, laid_1]
    )
    steps = [
        lamb_step(*entry)
        for entry in (
            (qkv_weight, grad_qkv, qkv_first, qkv_second, DECAY),
            (out_weight, grad_out, out_first, out_second, DECAY),
            (down_weight, grad_down, down_first, down_second, DECAY),
            (gain_weight, grad_gain, gain_first, gain_second, 0.0),
        )
    ]
    steps.insert(2, (gateup_one, gateup_two, gateup_update))
    new_ones, new_twos, updates = zip(*steps)

    def squares(arrays):
        return [jnp.sum(entry * entry) for entry in arrays]

    totals = [
        [*squares(entry[:2]), jnp.sum(gateup_sums[row]), *squares((entry[3], *entry[4]))]
        for row, entry in enumerate((masters, updates))
    ]

    def spots(entries):
        total = jnp.zeros((2, 6), F32)
        for row, column, value in entries:
            spot = np.zeros((2, 6), np.float32)
            spot[row, column] = 1.0
            total = total + value * spot
        return total

    entries = [
        (row, column, total)
        for row in range(2)
        for column, total in enumerate(totals[row])
    ]
    early = [entries[slot] for slot in (0, 1, 3, 4, 5, 6, 7, 9, 10, 11)]
    norms = lax.optimization_barrier(spots(early)) + spots([entries[2], entries[8]])
    norms = jnp.sqrt(butterfly(norms))
    ratios = norms[0] / norms[1]
    news = [masters[slot] - RATE * ratios[slot] * updates[slot] for slot in range(4)]
    news.append(masters[4] - RATE * ratios[4:6][:, None] * updates[4])
    copies = [entry.astype(BF) for entry in news]
    recent()
    return (output, input_grad, *news, *new_ones, *new_twos, *copies, norms)


def solution(mesh):
    rows, columns = P(("seq", "shard"), None), P(None, ("seq", "shard"))
    tokens = P("shard", "seq", None)
    states = (rows, rows, rows, rows, columns)
    return jax.shard_map(
        shards,
        mesh=mesh,
        in_specs=(tokens, tokens, P("shard", None)) + states * 3,
        out_specs=(tokens, tokens) + states * 4 + (P(),),
        check_vma=False,
    )
```

profile of v0, /device:TPU:0, one launch (start us, length us, event | category | flops | bytes accessed | tf_op | source)
XLA Modules:
  0.0 792.5 jit_solution(3344769615530805604)
XLA Ops:
  28.8 6.5 collective-permute-done.1
  37.7 6.7 collective-permute-done.4
  45.1 16.4 %collective-permute-done.5 = bf16[144,2560]{1,0:T(8,128)(2,1)} collective-permute-done((bf16[144,2560]{1,0:T(8,128)(2,1)}, bf16[144,2560]{1,0:T(8,128)(2,1)}, u32[]{:S(2)}, u32[]{:S(2)}) %collective-permute-start.5) | collective-permute-done | bytes 737312 | tf_op jit(solution)/shard_map/ppermute | solution.py:52
  78.9 11.6 %collective-permute-done.9 = bf16[144,2048]{1,0:T(8,128)(2,1)S(1)} collective-permute-done((bf16[144,2048]{1,0:T(8,128)(2,1)S(1)}, bf16[144,2048]{1,0:T(8,128)(2,1)S(1)}, u32[]{:S(2)}, u32[]{:S(2)}) %collective-permute-start.9) | collective-permute-done | bytes 589856 | tf_op jit(solution)/shard_map/ppermute | solution.py:52
  91.1 24.5 %collective-permute-done.8 = bf16[144,2048]{1,0:T(8,128)(2,1)} collective-permute-done((bf16[144,2048]{1,0:T(8,128)(2,1)}, bf16[144,2048]{1,0:T(8,128)(2,1)}, u32[]{:S(2)}, u32[]{:S(2)}) %collective-permute-start.8) | collective-permute-done | bytes 589856 | tf_op jit(solution)/shard_map/ppermute | solution.py:52
  124.5 4.7 all-gather.5.cloned.1.call-done.down_ref.right_ref
  138.7 5.0 collective-permute-start.12
  145.9 6.7 collective-permute-start.13
  155.1 6.2 collective-permute-done.12
  162.4 33.8 %collective-permute-done.13 = bf16[512,512]{1,0:T(8,128)(2,1)} collective-permute-done((bf16[512,512]{1,0:T(8,128)(2,1)}, bf16[512,512]{1,0:T(8,128)(2,1)}, u32[]{:S(2)}, u32[]{:S(2)}) %collective-permute-start.13) | collective-permute-done | bytes 524320 | tf_op jit(solution)/shard_map/ppermute | solution.py:52
  203.0 13.3 %collective-permute-start.15 = (bf16[64,2048]{1,0:T(8,128)(2,1)}, bf16[64,2048]{1,0:T(8,128)(2,1)}, u32[]{:S(2)}, u32[]{:S(2)}) collective-permute-start(bf16[64,2048]{1,0:T(8,128)(2,1)} %collective-permute-done.10), channel_id=1, source_target_pairs={{0,12},{1,13},{2,14},{3,15},{4,0},{5,1},{6,2},{7,3},{8,4},{9,5},{1... | collective-permute-start | bytes 786440 | tf_op jit(solution)/shard_map/ppermute | solution.py:52
  223.7 6.9 shard_map.461
  239.4 4.1 collective-permute-done.18
  247.7 6.4 collective-permute-start.21
  254.1 8.5 %collective-permute-done.19 = bf16[128,2048]{1,0:T(8,128)(2,1)S(1)} collective-permute-done((bf16[128,2048]{1,0:T(8,128)(2,1)}, bf16[128,2048]{1,0:T(8,128)(2,1)S(1)}, u32[]{:S(2)}, u32[]{:S(2)}) %collective-permute-start.19) | collective-permute-done | bytes 524320 | tf_op jit(solution)/shard_map/ppermute | solution.py:52
  262.6 15.0 %collective-permute-done.21 = bf16[128,2048]{1,0:T(8,128)(2,1)} collective-permute-done((bf16[128,2048]{1,0:T(8,128)(2,1)}, bf16[128,2048]{1,0:T(8,128)(2,1)}, u32[]{:S(2)}, u32[]{:S(2)}) %collective-permute-start.21) | collective-permute-done | bytes 524320 | tf_op jit(solution)/shard_map/ppermute | solution.py:52
  294.8 4.0 collective-permute-done.25
  298.9 19.6 %collective-permute-done.24 = bf16[128,2048]{1,0:T(8,128)(2,1)} collective-permute-done((bf16[128,2048]{1,0:T(8,128)(2,1)S(1)}, bf16[128,2048]{1,0:T(8,128)(2,1)}, u32[]{:S(2)}, u32[]{:S(2)}) %collective-permute-start.24) | collective-permute-done | bytes 524320 | tf_op jit(solution)/shard_map/ppermute | solution.py:52
  329.2 31.2 %shard_map.463 = (bf16[1024,1024]{1,0:T(8,128)(2,1)S(1)}, bf16[1024,1024]{1,0:T(8,128)(2,1)S(1)}, bf16[1024,1024]{1,0:T(8,128)(2,1)}, f32[512,2048]{1,0:T(8,128)}, bf16[512,2048]{1,0:T(8,128)(2,1)}) custom-call(bf16[1024,2048]{1,0:T(8,128)(2,1)} %copy-done, bf16[1024,2048]{1,0:T(8,128)(2,1)} %copy-done.3, bf16[2048,2048]{1,0:T(8,128)(2,1)} %bitcast.410, ...), custom_call_target="tpu_custom_call" | custom-call | flops 1000000000 | bytes 1 | tf_op jit(solution)/shard_map/pallas_call | solution.py:639
  360.9 4.0 collective-permute-done.28
  364.9 5.4 fusion.82
  371.4 9.8 %collective-permute-start.34 = (bf16[128,2048]{1,0:T(8,128)(2,1)}, bf16[128,2048]{1,0:T(8,128)(2,1)}, u32[]{:S(2)}, u32[]{:S(2)}) collective-permute-start(bf16[128,2048]{1,0:T(8,128)(2,1)} %get-tuple-element.277), channel_id=1, source_target_pairs={{0,12},{1,13},{2,14},{3,15},{4,0},{5,1},{6,2},{7,3},{8,4},{9,5},{1... | collective-permute-start | bytes 1572872 | tf_op jit(solution)/shard_map/ppermute | solution.py:52
  387.8 6.5 shard_map.464
  397.9 6.5 shard_map.466
  406.5 6.5 shard_map.465
  413.6 16.3 %collective-permute-done.33 = bf16[128,2048]{1,0:T(8,128)(2,1)} collective-permute-done((bf16[128,2048]{1,0:T(8,128)(2,1)}, bf16[128,2048]{1,0:T(8,128)(2,1)}, u32[]{:S(2)}, u32[]{:S(2)}) %collective-permute-start.33) | collective-permute-done | bytes 524320 | tf_op jit(solution)/shard_map/ppermute | solution.py:52
  434.3 9.0 %collective-permute-done.30 = bf16[512,1024]{1,0:T(8,128)(2,1)S(1)} collective-permute-done((bf16[512,1024]{1,0:T(8,128)(2,1)S(1)}, bf16[512,1024]{1,0:T(8,128)(2,1)S(1)}, u32[]{:S(2)}, u32[]{:S(2)}) %collective-permute-start.30) | collective-permute-done | bytes 1048608 | tf_op jit(solution)/shard_map/ppermute | solution.py:52
  453.1 6.2 collective-permute-done.38
  461.8 7.9 collective-permute-done.37
  472.6 7.3 collective-permute-done.41
  479.9 4.4 constant_dynamic-slice_fusion
  490.3 4.5 fusion.81
  498.4 13.6 %collective-permute-done.42 = bf16[128,2048]{1,0:T(8,128)(2,1)S(1)} collective-permute-done((bf16[128,2048]{1,0:T(8,128)(2,1)S(1)}, bf16[128,2048]{1,0:T(8,128)(2,1)S(1)}, u32[]{:S(2)}, u32[]{:S(2)}) %collective-permute-start.42) | collective-permute-done | bytes 524320 | tf_op jit(solution)/shard_map/ppermute | solution.py:52
  515.9 5.5 shard_map.468
  525.5 20.2 %shard_map.467 = (f32[4,128,2048]{2,1,0:T(8,128)}, bf16[4,128,2048]{2,1,0:T(8,128)(2,1)}, bf16[2048,512]{1,0:T(8,128)(2,1)}, bf16[256,2048]{1,0:T(8,128)(2,1)S(1)}, f32[1,2048]{1,0:T(1,128)S(1)}) custom-call(bf16[2,4,128,2048]{3,2,1,0:T(8,128)(2,1)} %bitcast.421, bf16[256,2048]{1,0:T(8,128)(2,1)} %bitcast.73.right_ref.out_ref, bf16[2048,512]{1,0:T(8,128)(2,1)} %bitcast.403, ...), custom_call_target="tpu_custom_call" | custom-call | flops 1000000000 | bytes 1 | tf_op jit(solution)/shard_map/pallas_call | solution.py:532
  569.7 4.4 collective-permute-start.53
  577.8 12.6 %collective-permute-done.51 = bf16[128,2048]{1,0:T(8,128)(2,1)S(1)} collective-permute-done((bf16[128,2048]{1,0:T(8,128)(2,1)S(1)}, bf16[128,2048]{1,0:T(8,128)(2,1)S(1)}, u32[]{:S(2)}, u32[]{:S(2)}) %collective-permute-start.51) | collective-permute-done | bytes 524320 | tf_op jit(solution)/shard_map/ppermute | solution.py:52
  592.2 5.8 collective-permute-start.55
  606.9 20.5 %collective-permute-done.54 = bf16[784,512]{1,0:T(8,128)(2,1)} collective-permute-done((bf16[784,512]{1,0:T(8,128)(2,1)}, bf16[784,512]{1,0:T(8,128)(2,1)}, u32[]{:S(2)}, u32[]{:S(2)}) %collective-permute-start.54) | collective-permute-done | bytes 802848 | tf_op jit(solution)/shard_map/ppermute | solution.py:52
  640.6 17.1 %collective-permute-start.58 = (bf16[144,512]{1,0:T(8,128)(2,1)S(1)}, bf16[144,512]{1,0:T(8,128)(2,1)S(1)}, u32[]{:S(2)}, u32[]{:S(2)}) collective-permute-start(bf16[144,512]{1,0:T(8,128)(2,1)S(1)} %pad_maximum_fusion.25), channel_id=1, source_target_pairs={{0,3},{1,2},{2,1},{3,0},{4,7},{5,6},{6,5},{7,4},{8,11},{9,10},{10,... | collective-permute-start | bytes 442376 | tf_op jit(solution)/shard_map/ppermute | solution.py:52
  663.8 13.0 %collective-permute-start.67 = (bf16[2,64,1024]{2,1,0:T(8,128)(2,1)}, bf16[2,64,1024]{2,1,0:T(8,128)(2,1)S(1)}, u32[]{:S(2)}, u32[]{:S(2)}) collective-permute-start(bf16[2,64,1024]{2,1,0:T(8,128)(2,1)} %get-tuple-element.297), channel_id=1, source_target_pairs={{0,4},{1,5},{2,6},{3,7},{4,8},{5,9},{6,10},{7,11},{8,12},{9,13},{1... | collective-permute-start | bytes 786440 | tf_op jit(solution)/shard_map/ppermute | solution.py:52
  677.5 11.0 %collective-permute-start.66 = (bf16[2,64,1024]{2,1,0:T(8,128)(2,1)}, bf16[2,64,1024]{2,1,0:T(8,128)(2,1)S(1)}, u32[]{:S(2)}, u32[]{:S(2)}) collective-permute-start(bf16[2,64,1024]{2,1,0:T(8,128)(2,1)} %get-tuple-element.298), channel_id=1, source_target_pairs={{0,8},{1,9},{2,10},{3,11},{4,12},{5,13},{6,14},{7,15},{8,0},{9,1},... | collective-permute-start | bytes 786440 | tf_op jit(solution)/shard_map/ppermute | solution.py:52
  695.0 6.6 collective-permute-done.65
  712.2 7.0 multiply_reduce_fusion.1
  728.5 6.6 multiply_add_fusion.4
  739.7 9.5 %shard_map.469 = (f32[64,16384]{1,0:T(8,128)}, f32[64,16384]{1,0:T(8,128)}, f32[64,16384]{1,0:T(8,128)S(1)}, f32[2,1024]{1,0:T(2,128)S(1)}) custom-call(f32[64,16384]{1,0:T(8,128)S(1)} %copy-done.2, f32[64,16384]{1,0:T(8,128)S(1)} %copy-done.14, f32[64,16384]{1,0:T(8,128)S(1)} %copy-done.15, bf16[2,4,64,1024]{3,2,1,0:T(8,128)(2,1)S(1)} %pad_maximum_fusion.10.first_ref, ...), custom_call_target="tpu_custom_call" | custom-call | flops 1000000000 | bytes 1 | tf_op jit(solution)/shard_map/pallas_call | solution.py:697
  751.2 5.1 collective-permute-start.69
  757.9 3.8 collective-permute-start.70
  (721 shorter events, 284.9 us)
Async XLA Ops:
  7.2 122.0 %all-gather.5.cloned.1.call-start = ((), (), s32[]{:S(2)}) async-start(), calls=%async_computation | async-start | bytes 5242880 | tf_op jit(solution)/shard_map/all_gather | solution.py:183
  7.2 57.4 %collective-permute-start.2 = (bf16[128,2048]{1,0:T(8,128)(2,1)}, bf16[128,2048]{1,0:T(8,128)(2,1)}, u32[]{:S(2)}, u32[]{:S(2)}) collective-permute-start(bf16[128,2048]{1,0:T(8,128)(2,1)} %bitcast.422), channel_id=1, source_target_pairs={{0,4},{1,5},{2,6},{3,7},{4,8},{5,9},{6,10},{7,11},{8,12},{9,13},{1... | collective-permute-start | bytes 1572872 | tf_op jit(solution)/shard_map/ppermute | solution.py:52
  10.3 24.9 %collective-permute-start.1 = (bf16[128,2048]{1,0:T(8,128)(2,1)}, bf16[128,2048]{1,0:T(8,128)(2,1)}, u32[]{:S(2)}, u32[]{:S(2)}) collective-permute-start(bf16[128,2048]{1,0:T(8,128)(2,1)} %bitcast.423), channel_id=1, source_target_pairs={{0,12},{1,13},{2,14},{3,15},{4,0},{5,1},{6,2},{7,3},{8,4},{9,5},{1... | collective-permute-start | bytes 1572872 | tf_op jit(solution)/shard_map/ppermute | solution.py:52
  19.0 45.6 %collective-permute-start = (bf16[64,8192]{1,0:T(8,128)(2,1)}, bf16[64,8192]{1,0:T(8,128)(2,1)}, u32[]{:S(2)}, u32[]{:S(2)}) collective-permute-start(bf16[64,8192]{1,0:T(8,128)(2,1)} %pad_maximum_fusion.9), channel_id=1, source_target_pairs={{0,16},{16,0},{1,17},{17,1},{2,18},{18,2},{3,19},{19,3},{4,20},{20... | collective-permute-start | bytes 3145736 | tf_op jit(solution)/shard_map/ppermute | solution.py:52
  27.2 34.3 %collective-permute-start.5 = (bf16[144,2560]{1,0:T(8,128)(2,1)}, bf16[144,2560]{1,0:T(8,128)(2,1)}, u32[]{:S(2)}, u32[]{:S(2)}) collective-permute-start(bf16[144,2560]{1,0:T(8,128)(2,1)} %get-tuple-element.324), channel_id=1, source_target_pairs={{0,2},{1,3},{2,0},{3,1},{4,6},{5,7},{6,4},{7,5},{8,10},{9,11},{10,... | collective-permute-start | bytes 2211848 | tf_op jit(solution)/shard_map/ppermute | solution.py:52
  35.2 29.4 %collective-permute-start.6 = (bf16[144,2560]{1,0:T(8,128)(2,1)}, bf16[144,2560]{1,0:T(8,128)(2,1)}, u32[]{:S(2)}, u32[]{:S(2)}) collective-permute-start(bf16[144,2560]{1,0:T(8,128)(2,1)} %get-tuple-element.98), channel_id=1, source_target_pairs={{0,3},{1,2},{2,1},{3,0},{4,7},{5,6},{6,5},{7,4},{8,11},{9,10},{10,... | collective-permute-start | bytes 2211848 | tf_op jit(solution)/shard_map/ppermute | solution.py:52
  64.7 224.1 %all-gather.7.cloned.1.call-start = ((), (), s32[]{:S(2)}) async-start(), calls=%async_computation.1 | async-start | bytes 10485760 | tf_op jit(solution)/shard_map/all_gather | solution.py:183
  73.1 42.5 %collective-permute-start.8 = (bf16[144,2048]{1,0:T(8,128)(2,1)}, bf16[144,2048]{1,0:T(8,128)(2,1)}, u32[]{:S(2)}, u32[]{:S(2)}) collective-permute-start(bf16[144,2048]{1,0:T(8,128)(2,1)} %get-tuple-element.339), channel_id=1, source_target_pairs={{0,8},{1,9},{2,10},{3,11},{4,12},{5,13},{6,14},{7,15},{8,0},{9,1},... | collective-permute-start | bytes 1769480 | tf_op jit(solution)/shard_map/ppermute | solution.py:52
  75.5 41.6 %collective-permute-start.7 = (bf16[144,2048]{1,0:T(8,128)(2,1)}, bf16[144,2048]{1,0:T(8,128)(2,1)}, u32[]{:S(2)}, u32[]{:S(2)}) collective-permute-start(bf16[144,2048]{1,0:T(8,128)(2,1)} %get-tuple-element.340), channel_id=1, source_target_pairs={{0,12},{1,13},{2,14},{3,15},{4,0},{5,1},{6,2},{7,3},{8,4},{9,5},{1... | collective-permute-start | bytes 1769480 | tf_op jit(solution)/shard_map/ppermute | solution.py:52
  77.5 47.0 %collective-permute-start.10 = (bf16[64,2048]{1,0:T(8,128)(2,1)S(1)}, bf16[64,2048]{1,0:T(8,128)(2,1)}, u32[]{:S(2)}, u32[]{:S(2)}) collective-permute-start(bf16[64,2048]{1,0:T(8,128)(2,1)S(1)} %copy-done.70), channel_id=1, source_target_pairs={{0,0},{1,4},{2,8},{3,12},{4,1},{5,5},{6,9},{7,13},{8,2},{9,6},{10,... | collective-permute-start | bytes 786440 | tf_op jit(solution)/shard_map/ppermute | solution.py:52
  135.8 62.6 %collective-permute-start.11 = (bf16[528,2048]{1,0:T(8,128)(2,1)}, bf16[528,2048]{1,0:T(8,128)(2,1)}, u32[]{:S(2)}, u32[]{:S(2)}) collective-permute-start(bf16[528,2048]{1,0:T(8,128)(2,1)} %constant_dynamic-update-slice_fusion), channel_id=1, source_target_pairs={{0,16},{16,0},{1,17},{17,1},{2,18},{18,2},{3,19},{19,3},{4,20},{20... | collective-permute-start | bytes 6488072 | tf_op jit(solution)/shard_map/ppermute | solution.py:52
  145.9 50.3 %collective-permute-start.13 = (bf16[512,512]{1,0:T(8,128)(2,1)}, bf16[512,512]{1,0:T(8,128)(2,1)}, u32[]{:S(2)}, u32[]{:S(2)}) collective-permute-start(bf16[512,512]{1,0:T(8,128)(2,1)} %bitcast.27), channel_id=1, source_target_pairs={{0,8},{1,9},{2,10},{3,11},{4,12},{5,13},{6,14},{7,15},{8,0},{9,1},... | collective-permute-start | bytes 1572872 | tf_op jit(solution)/shard_map/ppermute | solution.py:52
  152.6 44.7 %collective-permute-start.14 = (bf16[512,512]{1,0:T(8,128)(2,1)}, bf16[512,512]{1,0:T(8,128)(2,1)}, u32[]{:S(2)}, u32[]{:S(2)}) collective-permute-start(bf16[512,512]{1,0:T(8,128)(2,1)} %bitcast.27), channel_id=1, source_target_pairs={{0,4},{1,5},{2,6},{3,7},{4,8},{5,9},{6,10},{7,11},{8,12},{9,13},{1... | collective-permute-start | bytes 1572872 | tf_op jit(solution)/shard_map/ppermute | solution.py:52
  203.0 28.7 %collective-permute-start.17 = (bf16[64,2048]{1,0:T(8,128)(2,1)}, bf16[64,2048]{1,0:T(8,128)(2,1)S(1)}, u32[]{:S(2)}, u32[]{:S(2)}) collective-permute-start(bf16[64,2048]{1,0:T(8,128)(2,1)} %collective-permute-done.10), channel_id=1, source_target_pairs={{0,4},{1,5},{2,6},{3,7},{4,8},{5,9},{6,10},{7,11},{8,12},{9,13},{1... | collective-permute-start | bytes 786440 | tf_op jit(solution)/shard_map/ppermute | solution.py:52
  203.0 28.7 %collective-permute-start.16 = (bf16[64,2048]{1,0:T(8,128)(2,1)}, bf16[64,2048]{1,0:T(8,128)(2,1)}, u32[]{:S(2)}, u32[]{:S(2)}) collective-permute-start(bf16[64,2048]{1,0:T(8,128)(2,1)} %collective-permute-done.10), channel_id=1, source_target_pairs={{0,8},{1,9},{2,10},{3,11},{4,12},{5,13},{6,14},{7,15},{8,0},{9,1},... | collective-permute-start | bytes 786440 | tf_op jit(solution)/shard_map/ppermute | solution.py:52
  203.0 28.7 %collective-permute-start.15 = (bf16[64,2048]{1,0:T(8,128)(2,1)}, bf16[64,2048]{1,0:T(8,128)(2,1)}, u32[]{:S(2)}, u32[]{:S(2)}) collective-permute-start(bf16[64,2048]{1,0:T(8,128)(2,1)} %collective-permute-done.10), channel_id=1, source_target_pairs={{0,12},{1,13},{2,14},{3,15},{4,0},{5,1},{6,2},{7,3},{8,4},{9,5},{1... | collective-permute-start | bytes 786440 | tf_op jit(solution)/shard_map/ppermute | solution.py:52
  247.7 29.9 %collective-permute-start.21 = (bf16[128,2048]{1,0:T(8,128)(2,1)}, bf16[128,2048]{1,0:T(8,128)(2,1)}, u32[]{:S(2)}, u32[]{:S(2)}) collective-permute-start(bf16[128,2048]{1,0:T(8,128)(2,1)} %get-tuple-element.289), channel_id=1, source_target_pairs={{0,3},{1,2},{2,1},{3,0},{4,7},{5,6},{6,5},{7,4},{8,11},{9,10},{10,... | collective-permute-start | bytes 1572872 | tf_op jit(solution)/shard_map/ppermute | solution.py:52
  254.0 25.0 %collective-permute-start.20 = (bf16[128,2048]{1,0:T(8,128)(2,1)}, bf16[128,2048]{1,0:T(8,128)(2,1)}, u32[]{:S(2)}, u32[]{:S(2)}) collective-permute-start(bf16[128,2048]{1,0:T(8,128)(2,1)} %get-tuple-element.290), channel_id=1, source_target_pairs={{0,2},{1,3},{2,0},{3,1},{4,6},{5,7},{6,4},{7,5},{8,10},{9,11},{10,... | collective-permute-start | bytes 1572872 | tf_op jit(solution)/shard_map/ppermute | solution.py:52
  254.1 28.0 %collective-permute-start.22 = (bf16[128,2048]{1,0:T(8,128)(2,1)S(1)}, bf16[128,2048]{1,0:T(8,128)(2,1)S(1)}, u32[]{:S(2)}, u32[]{:S(2)}) collective-permute-start(bf16[128,2048]{1,0:T(8,128)(2,1)S(1)} %bitcast.424), channel_id=1, source_target_pairs={{0,8},{1,9},{2,10},{3,11},{4,12},{5,13},{6,14},{7,15},{8,0},{9,1},... | collective-permute-start | bytes 1572872 | tf_op jit(solution)/shard_map/ppermute | solution.py:52
  282.2 36.3 %collective-permute-start.24 = (bf16[128,2048]{1,0:T(8,128)(2,1)S(1)}, bf16[128,2048]{1,0:T(8,128)(2,1)}, u32[]{:S(2)}, u32[]{:S(2)}) collective-permute-start(bf16[128,2048]{1,0:T(8,128)(2,1)S(1)} %multiply_convert_fusion), channel_id=1, source_target_pairs={{0,8},{1,9},{2,10},{3,11},{4,12},{5,13},{6,14},{7,15},{8,0},{9,1},... | collective-permute-start | bytes 1572872 | tf_op jit(solution)/shard_map/ppermute | solution.py:52
  282.7 35.7 %collective-permute-start.23 = (bf16[128,2048]{1,0:T(8,128)(2,1)S(1)}, bf16[128,2048]{1,0:T(8,128)(2,1)}, u32[]{:S(2)}, u32[]{:S(2)}) collective-permute-start(bf16[128,2048]{1,0:T(8,128)(2,1)S(1)} %multiply_convert_fusion), channel_id=1, source_target_pairs={{0,12},{1,13},{2,14},{3,15},{4,0},{5,1},{6,2},{7,3},{8,4},{9,5},{1... | collective-permute-start | bytes 1572872 | tf_op jit(solution)/shard_map/ppermute | solution.py:52
  288.8 33.5 %collective-permute-start.27 = (bf16[512,2048]{1,0:T(8,128)(2,1)}, bf16[512,2048]{1,0:T(8,128)(2,1)}, u32[]{:S(2)}, u32[]{:S(2)}) collective-permute-start(bf16[512,2048]{1,0:T(8,128)(2,1)} %pad_maximum_fusion.3), channel_id=1, source_target_pairs={{0,16},{16,0},{1,17},{17,1},{2,18},{18,2},{3,19},{19,3},{4,20},{20... | collective-permute-start | bytes 6291464 | tf_op jit(solution)/shard_map/ppermute | solution.py:52
  371.4 41.5 %collective-permute-start.34 = (bf16[128,2048]{1,0:T(8,128)(2,1)}, bf16[128,2048]{1,0:T(8,128)(2,1)}, u32[]{:S(2)}, u32[]{:S(2)}) collective-permute-start(bf16[128,2048]{1,0:T(8,128)(2,1)} %get-tuple-element.277), channel_id=1, source_target_pairs={{0,12},{1,13},{2,14},{3,15},{4,0},{5,1},{6,2},{7,3},{8,4},{9,5},{1... | collective-permute-start | bytes 1572872 | tf_op jit(solution)/shard_map/ppermute | solution.py:52
  381.3 48.6 %collective-permute-start.33 = (bf16[128,2048]{1,0:T(8,128)(2,1)}, bf16[128,2048]{1,0:T(8,128)(2,1)}, u32[]{:S(2)}, u32[]{:S(2)}) collective-permute-start(bf16[128,2048]{1,0:T(8,128)(2,1)} %get-tuple-element.278), channel_id=1, source_target_pairs={{0,8},{1,9},{2,10},{3,11},{4,12},{5,13},{6,14},{7,15},{8,0},{9,1},... | collective-permute-start | bytes 1572872 | tf_op jit(solution)/shard_map/ppermute | solution.py:52
  383.7 46.2 %collective-permute-start.32 = (bf16[128,2048]{1,0:T(8,128)(2,1)}, bf16[128,2048]{1,0:T(8,128)(2,1)}, u32[]{:S(2)}, u32[]{:S(2)}) collective-permute-start(bf16[128,2048]{1,0:T(8,128)(2,1)} %get-tuple-element.279), channel_id=1, source_target_pairs={{0,4},{1,5},{2,6},{3,7},{4,8},{5,9},{6,10},{7,11},{8,12},{9,13},{1... | collective-permute-start | bytes 1572872 | tf_op jit(solution)/shard_map/ppermute | solution.py:52
  395.0 39.3 %collective-permute-start.31 = (bf16[512,1024]{1,0:T(8,128)(2,1)S(1)}, bf16[512,1024]{1,0:T(8,128)(2,1)S(1)}, u32[]{:S(2)}, u32[]{:S(2)}) collective-permute-start(bf16[512,1024]{1,0:T(8,128)(2,1)S(1)} %bitcast.438), channel_id=1, source_target_pairs={{0,3},{1,2},{2,1},{3,0},{4,7},{5,6},{6,5},{7,4},{8,11},{9,10},{10,... | collective-permute-start | bytes 3145736 | tf_op jit(solution)/shard_map/ppermute | solution.py:52
  396.5 46.9 %collective-permute-start.30 = (bf16[512,1024]{1,0:T(8,128)(2,1)S(1)}, bf16[512,1024]{1,0:T(8,128)(2,1)S(1)}, u32[]{:S(2)}, u32[]{:S(2)}) collective-permute-start(bf16[512,1024]{1,0:T(8,128)(2,1)S(1)} %bitcast.437), channel_id=1, source_target_pairs={{0,2},{1,3},{2,0},{3,1},{4,6},{5,7},{6,4},{7,5},{8,10},{9,11},{10,... | collective-permute-start | bytes 3145736 | tf_op jit(solution)/shard_map/ppermute | solution.py:52
  412.9 30.4 %collective-permute-start.29 = (bf16[512,1024]{1,0:T(8,128)(2,1)S(1)}, bf16[512,1024]{1,0:T(8,128)(2,1)S(1)}, u32[]{:S(2)}, u32[]{:S(2)}) collective-permute-start(bf16[512,1024]{1,0:T(8,128)(2,1)S(1)} %bitcast.436), channel_id=1, source_target_pairs={{0,1},{1,0},{2,3},{3,2},{4,5},{5,4},{6,7},{7,6},{8,9},{9,8},{10,11... | collective-permute-start | bytes 3145736 | tf_op jit(solution)/shard_map/ppermute | solution.py:52
  444.8 24.9 %collective-permute-start.37 = (bf16[128,2048]{1,0:T(8,128)(2,1)}, bf16[128,2048]{1,0:T(8,128)(2,1)}, u32[]{:S(2)}, u32[]{:S(2)}) collective-permute-start(bf16[128,2048]{1,0:T(8,128)(2,1)} %get-tuple-element.139), channel_id=1, source_target_pairs={{0,2},{1,3},{2,0},{3,1},{4,6},{5,7},{6,4},{7,5},{8,10},{9,11},{10,... | collective-permute-start | bytes 1572872 | tf_op jit(solution)/shard_map/ppermute | solution.py:52
  446.8 43.5 %collective-permute-start.35 = (bf16[512,2048]{1,0:T(8,128)(2,1)}, bf16[512,2048]{1,0:T(8,128)(2,1)}, u32[]{:S(2)}, u32[]{:S(2)}) collective-permute-start(bf16[512,2048]{1,0:T(8,128)(2,1)} %get-tuple-element.127), channel_id=1, source_target_pairs={{0,16},{16,0},{1,17},{17,1},{2,18},{18,2},{3,19},{19,3},{4,20},{20... | collective-permute-start | bytes 6291464 | tf_op jit(solution)/shard_map/ppermute | solution.py:52
  484.3 61.5 %collective-permute-start.47 = (bf16[512,1024]{1,0:T(8,128)(2,1)}, bf16[512,1024]{1,0:T(8,128)(2,1)}, u32[]{:S(2)}, u32[]{:S(2)}) collective-permute-start(bf16[512,1024]{1,0:T(8,128)(2,1)} %bitcast.103), channel_id=1, source_target_pairs={{0,2},{1,3},{2,0},{3,1},{4,6},{5,7},{6,4},{7,5},{8,10},{9,11},{10,... | collective-permute-start | bytes 3145736 | tf_op jit(solution)/shard_map/ppermute | solution.py:52
  485.6 60.1 %collective-permute-start.46 = (bf16[512,1024]{1,0:T(8,128)(2,1)}, bf16[512,1024]{1,0:T(8,128)(2,1)}, u32[]{:S(2)}, u32[]{:S(2)}) collective-permute-start(bf16[512,1024]{1,0:T(8,128)(2,1)} %bitcast.102), channel_id=1, source_target_pairs={{0,1},{1,0},{2,3},{3,2},{4,5},{5,4},{6,7},{7,6},{8,9},{9,8},{10,11... | collective-permute-start | bytes 3145736 | tf_op jit(solution)/shard_map/ppermute | solution.py:52
  488.0 26.6 %collective-permute-start.45 = (bf16[512,2048]{1,0:T(8,128)(2,1)S(1)}, bf16[512,2048]{1,0:T(8,128)(2,1)S(1)}, u32[]{:S(2)}, u32[]{:S(2)}) collective-permute-start(bf16[512,2048]{1,0:T(8,128)(2,1)S(1)} %pad_maximum_fusion.4), channel_id=1, source_target_pairs={{0,16},{16,0},{1,17},{17,1},{2,18},{18,2},{3,19},{19,3},{4,20},{20... | collective-permute-start | bytes 6291464 | tf_op jit(solution)/shard_map/ppermute | solution.py:52
  512.0 33.8 %collective-permute-start.48 = (bf16[512,1024]{1,0:T(8,128)(2,1)}, bf16[512,1024]{1,0:T(8,128)(2,1)}, u32[]{:S(2)}, u32[]{:S(2)}) collective-permute-start(bf16[512,1024]{1,0:T(8,128)(2,1)} %bitcast.104), channel_id=1, source_target_pairs={{0,3},{1,2},{2,1},{3,0},{4,7},{5,6},{6,5},{7,4},{8,11},{9,10},{10,... | collective-permute-start | bytes 3145736 | tf_op jit(solution)/shard_map/ppermute | solution.py:52
  514.5 31.3 %collective-permute-start.43 = (bf16[128,2048]{1,0:T(8,128)(2,1)}, bf16[128,2048]{1,0:T(8,128)(2,1)}, u32[]{:S(2)}, u32[]{:S(2)}) collective-permute-start(bf16[128,2048]{1,0:T(8,128)(2,1)} %get-tuple-element.137), channel_id=1, source_target_pairs={{0,8},{1,9},{2,10},{3,11},{4,12},{5,13},{6,14},{7,15},{8,0},{9,1},... | collective-permute-start | bytes 1572872 | tf_op jit(solution)/shard_map/ppermute | solution.py:52
  514.6 31.2 %collective-permute-start.44 = (bf16[128,2048]{1,0:T(8,128)(2,1)}, bf16[128,2048]{1,0:T(8,128)(2,1)}, u32[]{:S(2)}, u32[]{:S(2)}) collective-permute-start(bf16[128,2048]{1,0:T(8,128)(2,1)} %get-tuple-element.138), channel_id=1, source_target_pairs={{0,12},{1,13},{2,14},{3,15},{4,0},{5,1},{6,2},{7,3},{8,4},{9,5},{1... | collective-permute-start | bytes 1572872 | tf_op jit(solution)/shard_map/ppermute | solution.py:52
  565.1 25.3 %collective-permute-start.51 = (bf16[128,2048]{1,0:T(8,128)(2,1)S(1)}, bf16[128,2048]{1,0:T(8,128)(2,1)S(1)}, u32[]{:S(2)}, u32[]{:S(2)}) collective-permute-start(bf16[128,2048]{1,0:T(8,128)(2,1)S(1)} %get-tuple-element.152), channel_id=1, source_target_pairs={{0,2},{1,3},{2,0},{3,1},{4,6},{5,7},{6,4},{7,5},{8,10},{9,11},{10,... | collective-permute-start | bytes 1572872 | tf_op jit(solution)/shard_map/ppermute | solution.py:52
  569.7 36.2 %collective-permute-start.53 = (bf16[784,512]{1,0:T(8,128)(2,1)S(1)}, bf16[784,512]{1,0:T(8,128)(2,1)S(1)}, u32[]{:S(2)}, u32[]{:S(2)}) collective-permute-start(bf16[784,512]{1,0:T(8,128)(2,1)S(1)} %pad_maximum_fusion.15), channel_id=1, source_target_pairs={{0,4},{1,5},{2,6},{3,7},{4,8},{5,9},{6,10},{7,11},{8,12},{9,13},{1... | collective-permute-start | bytes 2408456 | tf_op jit(solution)/shard_map/ppermute | solution.py:52
  575.1 52.3 %collective-permute-start.54 = (bf16[784,512]{1,0:T(8,128)(2,1)}, bf16[784,512]{1,0:T(8,128)(2,1)}, u32[]{:S(2)}, u32[]{:S(2)}) collective-permute-start(bf16[784,512]{1,0:T(8,128)(2,1)} %pad_maximum_fusion.16), channel_id=1, source_target_pairs={{0,8},{1,9},{2,10},{3,11},{4,12},{5,13},{6,14},{7,15},{8,0},{9,1},... | collective-permute-start | bytes 2408456 | tf_op jit(solution)/shard_map/ppermute | solution.py:52
  592.2 39.2 %collective-permute-start.55 = (bf16[784,512]{1,0:T(8,128)(2,1)}, bf16[784,512]{1,0:T(8,128)(2,1)}, u32[]{:S(2)}, u32[]{:S(2)}) collective-permute-start(bf16[784,512]{1,0:T(8,128)(2,1)} %pad_maximum_fusion.17), channel_id=1, source_target_pairs={{0,12},{1,13},{2,14},{3,15},{4,0},{5,1},{6,2},{7,3},{8,4},{9,5},{1... | collective-permute-start | bytes 2408456 | tf_op jit(solution)/shard_map/ppermute | solution.py:52
  599.8 37.2 %collective-permute-start.57 = (bf16[256,2048]{1,0:T(8,128)(2,1)}, bf16[256,2048]{1,0:T(8,128)(2,1)}, u32[]{:S(2)}, u32[]{:S(2)}) collective-permute-start(bf16[256,2048]{1,0:T(8,128)(2,1)} %get-tuple-element.253), channel_id=1, source_target_pairs={{0,2},{1,3},{2,0},{3,1},{4,6},{5,7},{6,4},{7,5},{8,10},{9,11},{10,... | collective-permute-start | bytes 3145736 | tf_op jit(solution)/shard_map/ppermute | solution.py:52
  601.1 35.9 %collective-permute-start.56 = (bf16[256,2048]{1,0:T(8,128)(2,1)}, bf16[256,2048]{1,0:T(8,128)(2,1)}, u32[]{:S(2)}, u32[]{:S(2)}) collective-permute-start(bf16[256,2048]{1,0:T(8,128)(2,1)} %get-tuple-element.254), channel_id=1, source_target_pairs={{0,1},{1,0},{2,3},{3,2},{4,5},{5,4},{6,7},{7,6},{8,9},{9,8},{10,11... | collective-permute-start | bytes 3145736 | tf_op jit(solution)/shard_map/ppermute | solution.py:52
  628.1 84.1 %collective-permute-start.63 = (bf16[256,2048]{1,0:T(8,128)(2,1)}, bf16[256,2048]{1,0:T(8,128)(2,1)}, u32[]{:S(2)}, u32[]{:S(2)}) collective-permute-start(bf16[256,2048]{1,0:T(8,128)(2,1)} %get-tuple-element.163), channel_id=1, source_target_pairs={{0,3},{1,2},{2,1},{3,0},{4,7},{5,6},{6,5},{7,4},{8,11},{9,10},{10,... | collective-permute-start | bytes 3145736 | tf_op jit(solution)/shard_map/ppermute | solution.py:52
  637.0 72.3 %collective-permute-start.62 = (bf16[64,2048]{1,0:T(8,128)(2,1)}, bf16[64,2048]{1,0:T(8,128)(2,1)}, u32[]{:S(2)}, u32[]{:S(2)}) collective-permute-start(bf16[64,2048]{1,0:T(8,128)(2,1)} %convert_element_type.499), channel_id=1, source_target_pairs={{0,0},{1,4},{2,8},{3,12},{4,1},{5,5},{6,9},{7,13},{8,2},{9,6},{10,... | collective-permute-start | bytes 786440 | tf_op jit(solution)/shard_map/ppermute | solution.py:52
  658.5 30.7 %collective-permute-start.60 = (bf16[144,512]{1,0:T(8,128)(2,1)}, bf16[144,512]{1,0:T(8,128)(2,1)}, u32[]{:S(2)}, u32[]{:S(2)}) collective-permute-start(bf16[144,512]{1,0:T(8,128)(2,1)} %pad_maximum_fusion.27), channel_id=1, source_target_pairs={{0,1},{1,0},{2,3},{3,2},{4,5},{5,4},{6,7},{7,6},{8,9},{9,8},{10,11... | collective-permute-start | bytes 442376 | tf_op jit(solution)/shard_map/ppermute | solution.py:52
  663.8 39.3 %collective-permute-start.67 = (bf16[2,64,1024]{2,1,0:T(8,128)(2,1)}, bf16[2,64,1024]{2,1,0:T(8,128)(2,1)S(1)}, u32[]{:S(2)}, u32[]{:S(2)}) collective-permute-start(bf16[2,64,1024]{2,1,0:T(8,128)(2,1)} %get-tuple-element.297), channel_id=1, source_target_pairs={{0,4},{1,5},{2,6},{3,7},{4,8},{5,9},{6,10},{7,11},{8,12},{9,13},{1... | collective-permute-start | bytes 786440 | tf_op jit(solution)/shard_map/ppermute | solution.py:52
  677.5 24.9 %collective-permute-start.66 = (bf16[2,64,1024]{2,1,0:T(8,128)(2,1)}, bf16[2,64,1024]{2,1,0:T(8,128)(2,1)S(1)}, u32[]{:S(2)}, u32[]{:S(2)}) collective-permute-start(bf16[2,64,1024]{2,1,0:T(8,128)(2,1)} %get-tuple-element.298), channel_id=1, source_target_pairs={{0,8},{1,9},{2,10},{3,11},{4,12},{5,13},{6,14},{7,15},{8,0},{9,1},... | collective-permute-start | bytes 786440 | tf_op jit(solution)/shard_map/ppermute | solution.py:52
  708.7 26.3 %collective-permute-start.68 = (bf16[4,64,1024]{2,1,0:T(8,128)(2,1)}, bf16[4,64,1024]{2,1,0:T(8,128)(2,1)}, u32[]{:S(2)}, u32[]{:S(2)}) collective-permute-start(bf16[4,64,1024]{2,1,0:T(8,128)(2,1)} %dynamic-slice_bitcast_fusion.3), channel_id=1, source_target_pairs={{0,16},{16,0},{1,17},{17,1},{2,18},{18,2},{3,19},{19,3},{4,20},{20... | collective-permute-start | bytes 1572872 | tf_op jit(solution)/shard_map/ppermute | solution.py:52
  (162 other events, 1530.3 us)
Sparse Core Ops, SparseCore 0:
  64.8 64.3 all-gather.4
  131.6 95.6 all-gather.6
where the time goes:
time: 800 us; the launch traced here: 793 us
  waiting for transfers between devices  289 us (36%)
  starting transfers between devices  157 us (20%)
  local copies, waits for them, and re-layouts  121 us (15%)
  other arithmetic  110 us (14%)
  Pallas kernels  96.2 us (12%)
  between operations  19.8 us (2%)
    ppermute x74, waiting for transfers between devices, permute(): RECENT.append(lax.ppermute(values, axis, pairs))  284 us
    ppermute x74, starting transfers between devices, permute(): RECENT.append(lax.ppermute(values, axis, pairs))  157 us
    unnamed x326, local copies, waits for them, and re-layouts  54.1 us
    pallas_call x1, Pallas kernels, forward_back(): pl.pallas_call(forward_back_kernel, grid=(steps,), in_specs=[at_group((ro...  31.2 us
    pallas_call x1, Pallas kernels, attend_back(): pl.pallas_call(attend_back_kernel, grid=(groups,), in_specs=[at_group((2,...  20.2 us
    pallas_call x3, Pallas kernels, gradient(): pl.pallas_call(gradient_kernel, grid=(rows // block,), in_specs=[at_group...  18.5 us
    another operation x8, other arithmetic  17.6 us
  transfers between devices with their start and end apart: 76, of which 34 were waited for; matrix products, arithmetic and copies ran while one was open for 22% of the time, Pallas kernels for 7%

commit v1 on v0

--- a/solution.py
+++ b/solution.py
@@ -157,7 +157,7 @@
 
 
 def meet_halves(mine, other):
-    return jnp.split(mine + flip(other).astype(F32), TP)
+    return jnp.split(mine.astype(F32) + flip(other).astype(F32), TP)
 
 
 def gather_bits(own, low_bit, bits):
@@ -505,7 +505,7 @@
     columns.append(d_values.astype(BF))
     projected = jnp.concatenate(columns, axis=1)
     d_normed = dot_last(projected, qkv_ref[...])
-    mine_ref[0] = d_normed[: tokens // 2]
+    mine_ref[0] = d_normed[: tokens // 2].astype(BF)
     other_ref[0] = d_normed[tokens // 2 :].astype(BF)
 
     @pl.when(first)
@@ -556,7 +556,7 @@
             whole((1, width)),
         ],
         out_shape=[
-            jax.ShapeDtypeStruct((groups, half_tok, width), F32),
+            jax.ShapeDtypeStruct((groups, half_tok, width), BF),
             jax.ShapeDtypeStruct((groups, half_tok, width), BF),
             jax.ShapeDtypeStruct((width, HEAD_COLS), BF),
             jax.ShapeDtypeStruct((GROUP * HD, width), BF),
@@ -572,7 +572,7 @@
     first = pl.BlockSpec((rows, columns), lambda step: (jnp.minimum(step, steps // 2 - 1), 0))
     second = pl.BlockSpec((rows, columns), lambda step: (jnp.maximum(step - steps // 2, 0), 0))
     shapes = [
-        jax.ShapeDtypeStruct((rows * steps // 2, columns), F32),
+        jax.ShapeDtypeStruct((rows * steps // 2, columns), BF),
         jax.ShapeDtypeStruct((rows * steps // 2, columns), BF),
     ]
     return [first, second], shapes
@@ -583,7 +583,7 @@
 
     @pl.when(step < half)
     def _():
-        mine_ref[...] = values
+        mine_ref[...] = values.astype(BF)
 
     @pl.when(step >= half)
     def _():
@@ -844,18 +844,19 @@
     came = recent()
     held = after(total_0, *slot, d_branch_own)
     pieces = [column_piece(held, k) for k in range(TP)]
-    pieces[3] = after(pieces[3], *came)
-    laid_0 = lay_columns([from_column(pieces[k], k) for k in range(TP)])
     out_met = meet_halves(out_mine, after(out_other, *slot))
-    slot = (*came, *recent()[:3])
+    pieces[3] = after(pieces[3], *came, *recent())
+    pieces_0 = [from_column(pieces[k], k) for k in range(TP)]
+    slot = (*came, *recent())
 
     sends = [after(entry.astype(BF), *slot) for entry in out_met]
     result = middle + out_met[0]
     for k in range(1, TP):
-        result = result + to_column(sends[k], k).astype(F32)
+        send = sends[k] if k < 3 else after(sends[k], RECENT[0])
+        result = result + to_column(send, k).astype(F32)
     output = result.astype(BF)[None]
     out_came = recent()
-    parts_1 = place_parts(after(grad_half_1, *slot), rows, out_came[:1])
+    parts_1 = place_parts(after(grad_half_1, *slot), rows)
     out_came = (*out_came, *recent())
     d_branch = both_halves([after(entry, *slot) for entry in d_branch_mine])
     in_mine, in_other, grad_qkv, grad_out, d_gain_one = attend_back(
@@ -880,6 +881,8 @@
     for j in range(1, TP):
         d_normed = d_normed + from_corner(after(in_met[j].astype(BF), *slot), j).astype(F32)
     came = recent()
+    laid_0 = lay_columns([after(piece, *came) for piece in pieces_0])
+    recent()
     d_gains = jnp.concatenate([d_gain_one, d_gain_two[None]], axis=0)
     qkv_view = after(grad_qkv, *slot).reshape(2, place_size(), TP, rows, HEAD_COLS)
     out_view = after(grad_out, *slot).reshape(place_size(), -1, width)
@@ -911,10 +914,12 @@
     input_grad = (d_middle + d_in_part).astype(BF)[None]
 
     held = after(place_total([after(part, *came) for part in parts_1], rows), *slot)
-    laid_1 = lay_columns([from_column(column_piece(held, k), k) for k in range(TP)])
-    qkv_total = after(qkv_total.astype(BF), *slot).reshape(2, TP, rows, HEAD_COLS)
+    recent()
+    pieces_1 = [from_column(column_piece(held, k), k) for k in range(TP)]
+    qkv_total = after(qkv_total.astype(BF), *slot, *recent()).reshape(2, TP, rows, HEAD_COLS)
     grad_qkv, grad_gain = unspread_qkv(qkv_total, rows, rider)
     grad_qkv = grad_qkv.astype(F32)
+    laid_1 = lay_columns(pieces_1)
     grad_out = swap_roles(after(grad_out.astype(BF), *slot)).astype(F32)
     if not packed:
         grad_gain = lax.dynamic_slice_in_dim(butterfly(d_gains), owner * gain_cols, gain_cols, 1)

time: 800 us -> 769 us (0.961)
  waiting for transfers between devices: 289 us -> 270 us
    ppermute x74, waiting for transfers between devices: 284 us -> 265 us  [permute(): RECENT.append(lax.ppermute(values, axis, pairs))]
    another operation x8 -> x4, other arithmetic: 17.6 us -> 1.21 us
    add x0 -> x4, other arithmetic: none -> 12.8 us  [meet_halves(): return jnp.split(mine.astype(F32) + flip(other).astype(F32), TP)]
    unnamed x326 -> x340, local copies, waits for them, and re-layouts: 54.1 us -> 51.3 us
  transfers between devices with their start and end apart: 76 -> 76, of which waited for: 34 -> 35; matrix products, arithmetic and copies ran while one was open for 22% -> 22% of each run, Pallas kernels for 7% -> 7%
where the time goes in v1:
time: 769 us; the launch traced here: 760 us
  waiting for transfers between devices  270 us (35%)
  starting transfers between devices  151 us (20%)
  local copies, waits for them, and re-layouts  114 us (15%)
  other arithmetic  108 us (14%)
  Pallas kernels  96 us (12%)
  between operations  20.2 us (3%)
    ppermute x74, waiting for transfers between devices, permute(): RECENT.append(lax.ppermute(values, axis, pairs))  265 us
    ppermute x74, starting transfers between devices, permute(): RECENT.append(lax.ppermute(values, axis, pairs))  151 us
    unnamed x340, local copies, waits for them, and re-layouts  51.3 us
    pallas_call x1, Pallas kernels, forward_back(): pl.pallas_call(forward_back_kernel, grid=(steps,), in_specs=[at_group((ro...  30.8 us
    pallas_call x1, Pallas kernels, attend_back(): pl.pallas_call(attend_back_kernel, grid=(groups,), in_specs=[at_group((2,...  20.3 us
    pallas_call x3, Pallas kernels, gradient(): pl.pallas_call(gradient_kernel, grid=(rows // block,), in_specs=[at_group...  18.5 us
  transfers between devices with their start and end apart: 76, of which 35 were waited for; matrix products, arithmetic and copies ran while one was open for 22% of the time, Pallas kernels for 7%

profile of v1, /device:TPU:0, one launch (start us, length us, event | category | flops | bytes accessed | tf_op | source)
XLA Modules:
  0.0 759.5 jit_solution(2296394195358761875)
XLA Ops:
  28.8 6.5 collective-permute-done.1
  37.7 6.7 collective-permute-done.4
  45.1 16.4 %collective-permute-done.5 = bf16[144,2560]{1,0:T(8,128)(2,1)} collective-permute-done((bf16[144,2560]{1,0:T(8,128)(2,1)}, bf16[144,2560]{1,0:T(8,128)(2,1)}, u32[]{:S(2)}, u32[]{:S(2)}) %collective-permute-start.5) | collective-permute-done | bytes 737312 | tf_op jit(solution)/shard_map/ppermute | solution.py:52
  78.9 11.6 %collective-permute-done.9 = bf16[144,2048]{1,0:T(8,128)(2,1)S(1)} collective-permute-done((bf16[144,2048]{1,0:T(8,128)(2,1)S(1)}, bf16[144,2048]{1,0:T(8,128)(2,1)S(1)}, u32[]{:S(2)}, u32[]{:S(2)}) %collective-permute-start.9) | collective-permute-done | bytes 589856 | tf_op jit(solution)/shard_map/ppermute | solution.py:52
  91.1 24.5 %collective-permute-done.8 = bf16[144,2048]{1,0:T(8,128)(2,1)} collective-permute-done((bf16[144,2048]{1,0:T(8,128)(2,1)}, bf16[144,2048]{1,0:T(8,128)(2,1)}, u32[]{:S(2)}, u32[]{:S(2)}) %collective-permute-start.8) | collective-permute-done | bytes 589856 | tf_op jit(solution)/shard_map/ppermute | solution.py:52
  124.5 4.7 all-gather.5.cloned.1.call-done.down_ref.right_ref
  138.7 5.0 collective-permute-start.12
  145.9 6.7 collective-permute-start.13
  155.1 6.2 collective-permute-done.12
  162.4 33.8 %collective-permute-done.13 = bf16[512,512]{1,0:T(8,128)(2,1)} collective-permute-done((bf16[512,512]{1,0:T(8,128)(2,1)}, bf16[512,512]{1,0:T(8,128)(2,1)}, u32[]{:S(2)}, u32[]{:S(2)}) %collective-permute-start.13) | collective-permute-done | bytes 524320 | tf_op jit(solution)/shard_map/ppermute | solution.py:52
  203.0 4.3 collective-permute-start.15
  214.7 6.9 shard_map.461
  231.6 4.1 collective-permute-done.18
  239.9 5.2 collective-permute-start.21
  245.2 3.9 collective-permute-start.22
  249.0 5.8 collective-permute-done.19
  254.9 13.8 %collective-permute-done.21 = bf16[128,2048]{1,0:T(8,128)(2,1)} collective-permute-done((bf16[128,2048]{1,0:T(8,128)(2,1)}, bf16[128,2048]{1,0:T(8,128)(2,1)}, u32[]{:S(2)}, u32[]{:S(2)}) %collective-permute-start.21) | collective-permute-done | bytes 524320 | tf_op jit(solution)/shard_map/ppermute | solution.py:52
  273.2 4.9 collective-permute-start.25
  283.9 3.8 slice_bitcast_fusion
  290.0 3.6 collective-permute-done.25
  293.5 19.7 %collective-permute-done.24 = bf16[128,2048]{1,0:T(8,128)(2,1)} collective-permute-done((bf16[128,2048]{1,0:T(8,128)(2,1)S(1)}, bf16[128,2048]{1,0:T(8,128)(2,1)}, u32[]{:S(2)}, u32[]{:S(2)}) %collective-permute-start.24) | collective-permute-done | bytes 524320 | tf_op jit(solution)/shard_map/ppermute | solution.py:52
  324.0 30.8 %shard_map.463 = (bf16[1024,1024]{1,0:T(8,128)(2,1)S(1)}, bf16[1024,1024]{1,0:T(8,128)(2,1)S(1)}, bf16[1024,1024]{1,0:T(8,128)(2,1)}, bf16[512,2048]{1,0:T(8,128)(2,1)}, bf16[512,2048]{1,0:T(8,128)(2,1)}) custom-call(bf16[1024,2048]{1,0:T(8,128)(2,1)} %copy-done, bf16[1024,2048]{1,0:T(8,128)(2,1)} %copy-done.4, bf16[2048,2048]{1,0:T(8,128)(2,1)} %bitcast.414, ...), custom_call_target="tpu_custom_call" | custom-call | flops 1000000000 | bytes 1 | tf_op jit(solution)/shard_map/pallas_call | solution.py:639
  360.4 6.6 shard_map.464
  373.0 11.0 %collective-permute-start.34 = (bf16[128,2048]{1,0:T(8,128)(2,1)S(1)}, bf16[128,2048]{1,0:T(8,128)(2,1)S(1)}, u32[]{:S(2)}, u32[]{:S(2)}) collective-permute-start(bf16[128,2048]{1,0:T(8,128)(2,1)S(1)} %get-tuple-element.285), channel_id=1, source_target_pairs={{0,12},{1,13},{2,14},{3,15},{4,0},{5,1},{6,2},{7,3},{8,4},{9,5},{1... | collective-permute-start | bytes 1572872 | tf_op jit(solution)/shard_map/ppermute | solution.py:52
  388.4 8.2 %collective-permute-done.34 = bf16[128,2048]{1,0:T(8,128)(2,1)S(1)} collective-permute-done((bf16[128,2048]{1,0:T(8,128)(2,1)S(1)}, bf16[128,2048]{1,0:T(8,128)(2,1)S(1)}, u32[]{:S(2)}, u32[]{:S(2)}) %collective-permute-start.34) | collective-permute-done | bytes 524320 | tf_op jit(solution)/shard_map/ppermute | solution.py:52
  396.6 25.7 %collective-permute-start.32 = (bf16[128,2048]{1,0:T(8,128)(2,1)S(1)}, bf16[128,2048]{1,0:T(8,128)(2,1)S(1)}, u32[]{:S(2)}, u32[]{:S(2)}) collective-permute-start(bf16[128,2048]{1,0:T(8,128)(2,1)S(1)} %get-tuple-element.287), channel_id=1, source_target_pairs={{0,4},{1,5},{2,6},{3,7},{4,8},{5,9},{6,10},{7,11},{8,12},{9,13},{1... | collective-permute-start | bytes 1572872 | tf_op jit(solution)/shard_map/ppermute | solution.py:52
  422.2 6.4 shard_map.465
  431.6 6.5 shard_map.466
  449.9 7.9 %collective-permute-done.38 = bf16[128,2048]{1,0:T(8,128)(2,1)} collective-permute-done((bf16[128,2048]{1,0:T(8,128)(2,1)}, bf16[128,2048]{1,0:T(8,128)(2,1)}, u32[]{:S(2)}, u32[]{:S(2)}) %collective-permute-start.38) | collective-permute-done | bytes 524320 | tf_op jit(solution)/shard_map/ppermute | solution.py:52
  457.8 10.7 %collective-permute-done.37 = bf16[128,2048]{1,0:T(8,128)(2,1)} collective-permute-done((bf16[128,2048]{1,0:T(8,128)(2,1)}, bf16[128,2048]{1,0:T(8,128)(2,1)}, u32[]{:S(2)}, u32[]{:S(2)}) %collective-permute-start.37) | collective-permute-done | bytes 524320 | tf_op jit(solution)/shard_map/ppermute | solution.py:52
  468.6 10.0 %collective-permute-done.41 = bf16[2,64,1024]{2,1,0:T(8,128)(2,1)S(1)} collective-permute-done((bf16[2,64,1024]{2,1,0:T(8,128)(2,1)S(1)}, bf16[2,64,1024]{2,1,0:T(8,128)(2,1)S(1)}, u32[]{:S(2)}, u32[]{:S(2)}) %collective-permute-start.41) | collective-permute-done | bytes 262176 | tf_op jit(solution)/shard_map/ppermute | solution.py:52
  480.6 4.5 convert_add_fusion.1
  495.6 6.6 collective-permute-done.42
  504.4 5.4 shard_map.468
  514.0 20.3 %shard_map.467 = (bf16[4,128,2048]{2,1,0:T(8,128)(2,1)}, bf16[4,128,2048]{2,1,0:T(8,128)(2,1)}, bf16[2048,512]{1,0:T(8,128)(2,1)}, bf16[256,2048]{1,0:T(8,128)(2,1)S(1)}, f32[1,2048]{1,0:T(1,128)S(1)}) custom-call(bf16[2,4,128,2048]{3,2,1,0:T(8,128)(2,1)} %bitcast.422, bf16[256,2048]{1,0:T(8,128)(2,1)} %bitcast.73.right_ref.out_ref, ...), custom_call_target="tpu_custom_call" | custom-call | flops 1000000000 | bytes 1 | tf_op jit(solution)/shard_map/pallas_call | solution.py:532
  534.4 4.8 collective-permute-done.47
  557.9 3.7 collective-permute-start.54
  562.5 16.3 %collective-permute-done.51 = bf16[128,2048]{1,0:T(8,128)(2,1)S(1)} collective-permute-done((bf16[128,2048]{1,0:T(8,128)(2,1)S(1)}, bf16[128,2048]{1,0:T(8,128)(2,1)S(1)}, u32[]{:S(2)}, u32[]{:S(2)}) %collective-permute-start.51) | collective-permute-done | bytes 524320 | tf_op jit(solution)/shard_map/ppermute | solution.py:52
  595.2 18.5 %collective-permute-done.54 = bf16[784,512]{1,0:T(8,128)(2,1)} collective-permute-done((bf16[784,512]{1,0:T(8,128)(2,1)S(1)}, bf16[784,512]{1,0:T(8,128)(2,1)}, u32[]{:S(2)}, u32[]{:S(2)}) %collective-permute-start.54) | collective-permute-done | bytes 802848 | tf_op jit(solution)/shard_map/ppermute | solution.py:52
  622.8 13.9 %collective-permute-start.60 = (bf16[2,64,1024]{2,1,0:T(8,128)(2,1)}, bf16[2,64,1024]{2,1,0:T(8,128)(2,1)S(1)}, u32[]{:S(2)}, u32[]{:S(2)}) collective-permute-start(bf16[2,64,1024]{2,1,0:T(8,128)(2,1)} %get-tuple-element.313), channel_id=1, source_target_pairs={{0,4},{1,5},{2,6},{3,7},{4,8},{5,9},{6,10},{7,11},{8,12},{9,13},{1... | collective-permute-start | bytes 786440 | tf_op jit(solution)/shard_map/ppermute | solution.py:52
  645.9 11.3 %collective-permute-done.59 = bf16[2,64,1024]{2,1,0:T(8,128)(2,1)S(1)} collective-permute-done((bf16[2,64,1024]{2,1,0:T(8,128)(2,1)}, bf16[2,64,1024]{2,1,0:T(8,128)(2,1)S(1)}, u32[]{:S(2)}, u32[]{:S(2)}) %collective-permute-start.59) | collective-permute-done | bytes 262176 | tf_op jit(solution)/shard_map/ppermute | solution.py:52
  657.1 4.0 collective-permute-done.58
  677.5 8.2 %multiply_reduce_fusion.1 = (f32[]{:T(128)}, f32[]{:T(128)}, f32[256,2048]{1,0:T(8,128)}, f32[256,2048]{1,0:T(8,128)}) fusion(f32[256,2048]{1,0:T(8,128)S(1)} %copy-done.33, bf16[256,2048]{1,0:T(8,128)(2,1)} %collective-permute-done.66, bf16[256,2048]{1,0:T(8,128)(2,1)} %collective-permute-done.57, bf16[256,2048]{1,0:T(8,128)(2,1)} %collective-permute-done.56, ...), kind=kLoop, calls=%fused_computation.33 | loop fusion | flops 12582910 | bytes 14680076 | tf_op jit(solution)/shard_map/reduce_sum | solution.py:944
  691.4 3.5 multiply_reduce_fusion.4
  695.0 6.4 multiply_add_fusion.4
  706.2 9.5 %shard_map.469 = (f32[64,16384]{1,0:T(8,128)}, f32[64,16384]{1,0:T(8,128)}, f32[64,16384]{1,0:T(8,128)S(1)}, f32[2,1024]{1,0:T(2,128)S(1)}) custom-call(f32[64,16384]{1,0:T(8,128)S(1)} %copy-done.3, f32[64,16384]{1,0:T(8,128)S(1)} %copy-done.16, f32[64,16384]{1,0:T(8,128)S(1)} %copy-done.17, bf16[2,4,64,1024]{3,2,1,0:T(8,128)(2,1)S(1)} %pad_maximum_fusion.10.first_ref, ...), custom_call_target="tpu_custom_call" | custom-call | flops 1000000000 | bytes 1 | tf_op jit(solution)/shard_map/pallas_call | solution.py:697
  717.6 4.7 collective-permute-start.69
  723.8 4.4 collective-permute-start.70
  (735 shorter events, 271.2 us)
Async XLA Ops:
  7.2 122.0 %all-gather.5.cloned.1.call-start = ((), (), s32[]{:S(2)}) async-start(), calls=%async_computation | async-start | bytes 5242880 | tf_op jit(solution)/shard_map/all_gather | solution.py:183
  7.2 57.4 %collective-permute-start.2 = (bf16[128,2048]{1,0:T(8,128)(2,1)}, bf16[128,2048]{1,0:T(8,128)(2,1)}, u32[]{:S(2)}, u32[]{:S(2)}) collective-permute-start(bf16[128,2048]{1,0:T(8,128)(2,1)} %bitcast.423), channel_id=1, source_target_pairs={{0,4},{1,5},{2,6},{3,7},{4,8},{5,9},{6,10},{7,11},{8,12},{9,13},{1... | collective-permute-start | bytes 1572872 | tf_op jit(solution)/shard_map/ppermute | solution.py:52
  10.3 24.9 %collective-permute-start.1 = (bf16[128,2048]{1,0:T(8,128)(2,1)}, bf16[128,2048]{1,0:T(8,128)(2,1)}, u32[]{:S(2)}, u32[]{:S(2)}) collective-permute-start(bf16[128,2048]{1,0:T(8,128)(2,1)} %bitcast.424), channel_id=1, source_target_pairs={{0,12},{1,13},{2,14},{3,15},{4,0},{5,1},{6,2},{7,3},{8,4},{9,5},{1... | collective-permute-start | bytes 1572872 | tf_op jit(solution)/shard_map/ppermute | solution.py:52
  19.0 45.6 %collective-permute-start = (bf16[64,8192]{1,0:T(8,128)(2,1)}, bf16[64,8192]{1,0:T(8,128)(2,1)}, u32[]{:S(2)}, u32[]{:S(2)}) collective-permute-start(bf16[64,8192]{1,0:T(8,128)(2,1)} %pad_maximum_fusion.9), channel_id=1, source_target_pairs={{0,16},{16,0},{1,17},{17,1},{2,18},{18,2},{3,19},{19,3},{4,20},{20... | collective-permute-start | bytes 3145736 | tf_op jit(solution)/shard_map/ppermute | solution.py:52
  27.2 34.3 %collective-permute-start.5 = (bf16[144,2560]{1,0:T(8,128)(2,1)}, bf16[144,2560]{1,0:T(8,128)(2,1)}, u32[]{:S(2)}, u32[]{:S(2)}) collective-permute-start(bf16[144,2560]{1,0:T(8,128)(2,1)} %get-tuple-element.333), channel_id=1, source_target_pairs={{0,2},{1,3},{2,0},{3,1},{4,6},{5,7},{6,4},{7,5},{8,10},{9,11},{10,... | collective-permute-start | bytes 2211848 | tf_op jit(solution)/shard_map/ppermute | solution.py:52
  35.2 29.4 %collective-permute-start.6 = (bf16[144,2560]{1,0:T(8,128)(2,1)}, bf16[144,2560]{1,0:T(8,128)(2,1)}, u32[]{:S(2)}, u32[]{:S(2)}) collective-permute-start(bf16[144,2560]{1,0:T(8,128)(2,1)} %get-tuple-element.102), channel_id=1, source_target_pairs={{0,3},{1,2},{2,1},{3,0},{4,7},{5,6},{6,5},{7,4},{8,11},{9,10},{10,... | collective-permute-start | bytes 2211848 | tf_op jit(solution)/shard_map/ppermute | solution.py:52
  64.7 219.2 %all-gather.7.cloned.1.call-start = ((), (), s32[]{:S(2)}) async-start(), calls=%async_computation.1 | async-start | bytes 10485760 | tf_op jit(solution)/shard_map/all_gather | solution.py:183
  73.1 42.5 %collective-permute-start.8 = (bf16[144,2048]{1,0:T(8,128)(2,1)}, bf16[144,2048]{1,0:T(8,128)(2,1)}, u32[]{:S(2)}, u32[]{:S(2)}) collective-permute-start(bf16[144,2048]{1,0:T(8,128)(2,1)} %get-tuple-element.348), channel_id=1, source_target_pairs={{0,8},{1,9},{2,10},{3,11},{4,12},{5,13},{6,14},{7,15},{8,0},{9,1},... | collective-permute-start | bytes 1769480 | tf_op jit(solution)/shard_map/ppermute | solution.py:52
  75.5 41.6 %collective-permute-start.7 = (bf16[144,2048]{1,0:T(8,128)(2,1)}, bf16[144,2048]{1,0:T(8,128)(2,1)}, u32[]{:S(2)}, u32[]{:S(2)}) collective-permute-start(bf16[144,2048]{1,0:T(8,128)(2,1)} %get-tuple-element.349), channel_id=1, source_target_pairs={{0,12},{1,13},{2,14},{3,15},{4,0},{5,1},{6,2},{7,3},{8,4},{9,5},{1... | collective-permute-start | bytes 1769480 | tf_op jit(solution)/shard_map/ppermute | solution.py:52
  77.6 46.9 %collective-permute-start.10 = (bf16[64,2048]{1,0:T(8,128)(2,1)S(1)}, bf16[64,2048]{1,0:T(8,128)(2,1)}, u32[]{:S(2)}, u32[]{:S(2)}) collective-permute-start(bf16[64,2048]{1,0:T(8,128)(2,1)S(1)} %copy-done.79), channel_id=1, source_target_pairs={{0,0},{1,4},{2,8},{3,12},{4,1},{5,5},{6,9},{7,13},{8,2},{9,6},{10,... | collective-permute-start | bytes 786440 | tf_op jit(solution)/shard_map/ppermute | solution.py:52
  135.8 62.6 %collective-permute-start.11 = (bf16[528,2048]{1,0:T(8,128)(2,1)}, bf16[528,2048]{1,0:T(8,128)(2,1)}, u32[]{:S(2)}, u32[]{:S(2)}) collective-permute-start(bf16[528,2048]{1,0:T(8,128)(2,1)} %constant_dynamic-update-slice_fusion), channel_id=1, source_target_pairs={{0,16},{16,0},{1,17},{17,1},{2,18},{18,2},{3,19},{19,3},{4,20},{20... | collective-permute-start | bytes 6488072 | tf_op jit(solution)/shard_map/ppermute | solution.py:52
  138.7 22.7 %collective-permute-start.12 = (bf16[512,512]{1,0:T(8,128)(2,1)}, bf16[512,512]{1,0:T(8,128)(2,1)}, u32[]{:S(2)}, u32[]{:S(2)}) collective-permute-start(bf16[512,512]{1,0:T(8,128)(2,1)} %bitcast.27), channel_id=1, source_target_pairs={{0,12},{1,13},{2,14},{3,15},{4,0},{5,1},{6,2},{7,3},{8,4},{9,5},{1... | collective-permute-start | bytes 1572872 | tf_op jit(solution)/shard_map/ppermute | solution.py:52
  145.9 50.3 %collective-permute-start.13 = (bf16[512,512]{1,0:T(8,128)(2,1)}, bf16[512,512]{1,0:T(8,128)(2,1)}, u32[]{:S(2)}, u32[]{:S(2)}) collective-permute-start(bf16[512,512]{1,0:T(8,128)(2,1)} %bitcast.27), channel_id=1, source_target_pairs={{0,8},{1,9},{2,10},{3,11},{4,12},{5,13},{6,14},{7,15},{8,0},{9,1},... | collective-permute-start | bytes 1572872 | tf_op jit(solution)/shard_map/ppermute | solution.py:52
  152.6 44.7 %collective-permute-start.14 = (bf16[512,512]{1,0:T(8,128)(2,1)}, bf16[512,512]{1,0:T(8,128)(2,1)}, u32[]{:S(2)}, u32[]{:S(2)}) collective-permute-start(bf16[512,512]{1,0:T(8,128)(2,1)} %bitcast.27), channel_id=1, source_target_pairs={{0,4},{1,5},{2,6},{3,7},{4,8},{5,9},{6,10},{7,11},{8,12},{9,13},{1... | collective-permute-start | bytes 1572872 | tf_op jit(solution)/shard_map/ppermute | solution.py:52
  239.9 28.8 %collective-permute-start.21 = (bf16[128,2048]{1,0:T(8,128)(2,1)}, bf16[128,2048]{1,0:T(8,128)(2,1)}, u32[]{:S(2)}, u32[]{:S(2)}) collective-permute-start(bf16[128,2048]{1,0:T(8,128)(2,1)} %get-tuple-element.297), channel_id=1, source_target_pairs={{0,3},{1,2},{2,1},{3,0},{4,7},{5,6},{6,5},{7,4},{8,11},{9,10},{10,... | collective-permute-start | bytes 1572872 | tf_op jit(solution)/shard_map/ppermute | solution.py:52
  245.1 25.0 %collective-permute-start.20 = (bf16[128,2048]{1,0:T(8,128)(2,1)}, bf16[128,2048]{1,0:T(8,128)(2,1)}, u32[]{:S(2)}, u32[]{:S(2)}) collective-permute-start(bf16[128,2048]{1,0:T(8,128)(2,1)} %get-tuple-element.298), channel_id=1, source_target_pairs={{0,2},{1,3},{2,0},{3,1},{4,6},{5,7},{6,4},{7,5},{8,10},{9,11},{10,... | collective-permute-start | bytes 1572872 | tf_op jit(solution)/shard_map/ppermute | solution.py:52
  245.2 28.0 %collective-permute-start.22 = (bf16[128,2048]{1,0:T(8,128)(2,1)S(1)}, bf16[128,2048]{1,0:T(8,128)(2,1)S(1)}, u32[]{:S(2)}, u32[]{:S(2)}) collective-permute-start(bf16[128,2048]{1,0:T(8,128)(2,1)S(1)} %bitcast.425), channel_id=1, source_target_pairs={{0,8},{1,9},{2,10},{3,11},{4,12},{5,13},{6,14},{7,15},{8,0},{9,1},... | collective-permute-start | bytes 1572872 | tf_op jit(solution)/shard_map/ppermute | solution.py:52
  278.1 35.2 %collective-permute-start.24 = (bf16[128,2048]{1,0:T(8,128)(2,1)S(1)}, bf16[128,2048]{1,0:T(8,128)(2,1)}, u32[]{:S(2)}, u32[]{:S(2)}) collective-permute-start(bf16[128,2048]{1,0:T(8,128)(2,1)S(1)} %multiply_convert_fusion), channel_id=1, source_target_pairs={{0,8},{1,9},{2,10},{3,11},{4,12},{5,13},{6,14},{7,15},{8,0},{9,1},... | collective-permute-start | bytes 1572872 | tf_op jit(solution)/shard_map/ppermute | solution.py:52
  281.2 32.1 %collective-permute-start.23 = (bf16[128,2048]{1,0:T(8,128)(2,1)S(1)}, bf16[128,2048]{1,0:T(8,128)(2,1)}, u32[]{:S(2)}, u32[]{:S(2)}) collective-permute-start(bf16[128,2048]{1,0:T(8,128)(2,1)S(1)} %multiply_convert_fusion), channel_id=1, source_target_pairs={{0,12},{1,13},{2,14},{3,15},{4,0},{5,1},{6,2},{7,3},{8,4},{9,5},{1... | collective-permute-start | bytes 1572872 | tf_op jit(solution)/shard_map/ppermute | solution.py:52
  283.9 33.2 %collective-permute-start.27 = (bf16[512,2048]{1,0:T(8,128)(2,1)}, bf16[512,2048]{1,0:T(8,128)(2,1)}, u32[]{:S(2)}, u32[]{:S(2)}) collective-permute-start(bf16[512,2048]{1,0:T(8,128)(2,1)} %pad_maximum_fusion.3), channel_id=1, source_target_pairs={{0,16},{16,0},{1,17},{17,1},{2,18},{18,2},{3,19},{19,3},{4,20},{20... | collective-permute-start | bytes 6291464 | tf_op jit(solution)/shard_map/ppermute | solution.py:52
  368.7 62.8 %collective-permute-start.31 = (bf16[512,1024]{1,0:T(8,128)(2,1)S(1)}, bf16[512,1024]{1,0:T(8,128)(2,1)S(1)}, u32[]{:S(2)}, u32[]{:S(2)}) collective-permute-start(bf16[512,1024]{1,0:T(8,128)(2,1)S(1)} %bitcast.440), channel_id=1, source_target_pairs={{0,3},{1,2},{2,1},{3,0},{4,7},{5,6},{6,5},{7,4},{8,11},{9,10},{10,... | collective-permute-start | bytes 3145736 | tf_op jit(solution)/shard_map/ppermute | solution.py:52
  373.0 23.5 %collective-permute-start.34 = (bf16[128,2048]{1,0:T(8,128)(2,1)S(1)}, bf16[128,2048]{1,0:T(8,128)(2,1)S(1)}, u32[]{:S(2)}, u32[]{:S(2)}) collective-permute-start(bf16[128,2048]{1,0:T(8,128)(2,1)S(1)} %get-tuple-element.285), channel_id=1, source_target_pairs={{0,12},{1,13},{2,14},{3,15},{4,0},{5,1},{6,2},{7,3},{8,4},{9,5},{1... | collective-permute-start | bytes 1572872 | tf_op jit(solution)/shard_map/ppermute | solution.py:52
  384.1 47.4 %collective-permute-start.30 = (bf16[512,1024]{1,0:T(8,128)(2,1)S(1)}, bf16[512,1024]{1,0:T(8,128)(2,1)S(1)}, u32[]{:S(2)}, u32[]{:S(2)}) collective-permute-start(bf16[512,1024]{1,0:T(8,128)(2,1)S(1)} %bitcast.439), channel_id=1, source_target_pairs={{0,2},{1,3},{2,0},{3,1},{4,6},{5,7},{6,4},{7,5},{8,10},{9,11},{10,... | collective-permute-start | bytes 3145736 | tf_op jit(solution)/shard_map/ppermute | solution.py:52
  385.5 46.0 %collective-permute-start.29 = (bf16[512,1024]{1,0:T(8,128)(2,1)S(1)}, bf16[512,1024]{1,0:T(8,128)(2,1)S(1)}, u32[]{:S(2)}, u32[]{:S(2)}) collective-permute-start(bf16[512,1024]{1,0:T(8,128)(2,1)S(1)} %bitcast.438), channel_id=1, source_target_pairs={{0,1},{1,0},{2,3},{3,2},{4,5},{5,4},{6,7},{7,6},{8,9},{9,8},{10,11... | collective-permute-start | bytes 3145736 | tf_op jit(solution)/shard_map/ppermute | solution.py:52
  386.2 45.3 %collective-permute-start.33 = (bf16[128,2048]{1,0:T(8,128)(2,1)S(1)}, bf16[128,2048]{1,0:T(8,128)(2,1)S(1)}, u32[]{:S(2)}, u32[]{:S(2)}) collective-permute-start(bf16[128,2048]{1,0:T(8,128)(2,1)S(1)} %get-tuple-element.286), channel_id=1, source_target_pairs={{0,8},{1,9},{2,10},{3,11},{4,12},{5,13},{6,14},{7,15},{8,0},{9,1},... | collective-permute-start | bytes 1572872 | tf_op jit(solution)/shard_map/ppermute | solution.py:52
  396.6 34.9 %collective-permute-start.32 = (bf16[128,2048]{1,0:T(8,128)(2,1)S(1)}, bf16[128,2048]{1,0:T(8,128)(2,1)S(1)}, u32[]{:S(2)}, u32[]{:S(2)}) collective-permute-start(bf16[128,2048]{1,0:T(8,128)(2,1)S(1)} %get-tuple-element.287), channel_id=1, source_target_pairs={{0,4},{1,5},{2,6},{3,7},{4,8},{5,9},{6,10},{7,11},{8,12},{9,13},{1... | collective-permute-start | bytes 1572872 | tf_op jit(solution)/shard_map/ppermute | solution.py:52
  431.5 37.1 %collective-permute-start.35 = (bf16[512,2048]{1,0:T(8,128)(2,1)}, bf16[512,2048]{1,0:T(8,128)(2,1)}, u32[]{:S(2)}, u32[]{:S(2)}) collective-permute-start(bf16[512,2048]{1,0:T(8,128)(2,1)} %get-tuple-element.131), channel_id=1, source_target_pairs={{0,16},{16,0},{1,17},{17,1},{2,18},{18,2},{3,19},{19,3},{4,20},{20... | collective-permute-start | bytes 6291464 | tf_op jit(solution)/shard_map/ppermute | solution.py:52
  443.3 25.2 %collective-permute-start.37 = (bf16[128,2048]{1,0:T(8,128)(2,1)}, bf16[128,2048]{1,0:T(8,128)(2,1)}, u32[]{:S(2)}, u32[]{:S(2)}) collective-permute-start(bf16[128,2048]{1,0:T(8,128)(2,1)} %get-tuple-element.144), channel_id=1, source_target_pairs={{0,2},{1,3},{2,0},{3,1},{4,6},{5,7},{6,4},{7,5},{8,10},{9,11},{10,... | collective-permute-start | bytes 1572872 | tf_op jit(solution)/shard_map/ppermute | solution.py:52
  444.7 23.9 %collective-permute-start.36 = (bf16[128,2048]{1,0:T(8,128)(2,1)}, bf16[128,2048]{1,0:T(8,128)(2,1)}, u32[]{:S(2)}, u32[]{:S(2)}) collective-permute-start(bf16[128,2048]{1,0:T(8,128)(2,1)} %get-tuple-element.144), channel_id=1, source_target_pairs={{0,1},{1,0},{2,3},{3,2},{4,5},{5,4},{6,7},{7,6},{8,9},{9,8},{10,11... | collective-permute-start | bytes 1572872 | tf_op jit(solution)/shard_map/ppermute | solution.py:52
  489.9 44.4 %collective-permute-start.48 = (bf16[512,1024]{1,0:T(8,128)(2,1)}, bf16[512,1024]{1,0:T(8,128)(2,1)}, u32[]{:S(2)}, u32[]{:S(2)}) collective-permute-start(bf16[512,1024]{1,0:T(8,128)(2,1)} %bitcast.104), channel_id=1, source_target_pairs={{0,3},{1,2},{2,1},{3,0},{4,7},{5,6},{6,5},{7,4},{8,11},{9,10},{10,... | collective-permute-start | bytes 3145736 | tf_op jit(solution)/shard_map/ppermute | solution.py:52
  491.5 47.7 %collective-permute-start.47 = (bf16[512,1024]{1,0:T(8,128)(2,1)}, bf16[512,1024]{1,0:T(8,128)(2,1)}, u32[]{:S(2)}, u32[]{:S(2)}) collective-permute-start(bf16[512,1024]{1,0:T(8,128)(2,1)} %bitcast.103), channel_id=1, source_target_pairs={{0,2},{1,3},{2,0},{3,1},{4,6},{5,7},{6,4},{7,5},{8,10},{9,11},{10,... | collective-permute-start | bytes 3145736 | tf_op jit(solution)/shard_map/ppermute | solution.py:52
  492.8 46.4 %collective-permute-start.46 = (bf16[512,1024]{1,0:T(8,128)(2,1)}, bf16[512,1024]{1,0:T(8,128)(2,1)}, u32[]{:S(2)}, u32[]{:S(2)}) collective-permute-start(bf16[512,1024]{1,0:T(8,128)(2,1)} %bitcast.102), channel_id=1, source_target_pairs={{0,1},{1,0},{2,3},{3,2},{4,5},{5,4},{6,7},{7,6},{8,9},{9,8},{10,11... | collective-permute-start | bytes 3145736 | tf_op jit(solution)/shard_map/ppermute | solution.py:52
  502.2 32.1 %collective-permute-start.43 = (bf16[128,2048]{1,0:T(8,128)(2,1)}, bf16[128,2048]{1,0:T(8,128)(2,1)}, u32[]{:S(2)}, u32[]{:S(2)}) collective-permute-start(bf16[128,2048]{1,0:T(8,128)(2,1)} %get-tuple-element.141), channel_id=1, source_target_pairs={{0,8},{1,9},{2,10},{3,11},{4,12},{5,13},{6,14},{7,15},{8,0},{9,1},... | collective-permute-start | bytes 1572872 | tf_op jit(solution)/shard_map/ppermute | solution.py:52
  502.2 37.0 %collective-permute-start.44 = (bf16[128,2048]{1,0:T(8,128)(2,1)S(1)}, bf16[128,2048]{1,0:T(8,128)(2,1)}, u32[]{:S(2)}, u32[]{:S(2)}) collective-permute-start(bf16[128,2048]{1,0:T(8,128)(2,1)S(1)} %get-tuple-element.143), channel_id=1, source_target_pairs={{0,12},{1,13},{2,14},{3,15},{4,0},{5,1},{6,2},{7,3},{8,4},{9,5},{1... | collective-permute-start | bytes 1572872 | tf_op jit(solution)/shard_map/ppermute | solution.py:52
  553.2 25.6 %collective-permute-start.51 = (bf16[128,2048]{1,0:T(8,128)(2,1)S(1)}, bf16[128,2048]{1,0:T(8,128)(2,1)S(1)}, u32[]{:S(2)}, u32[]{:S(2)}) collective-permute-start(bf16[128,2048]{1,0:T(8,128)(2,1)S(1)} %get-tuple-element.156), channel_id=1, source_target_pairs={{0,2},{1,3},{2,0},{3,1},{4,6},{5,7},{6,4},{7,5},{8,10},{9,11},{10,... | collective-permute-start | bytes 1572872 | tf_op jit(solution)/shard_map/ppermute | solution.py:52
  554.7 24.1 %collective-permute-start.52 = (bf16[128,2048]{1,0:T(8,128)(2,1)S(1)}, bf16[128,2048]{1,0:T(8,128)(2,1)S(1)}, u32[]{:S(2)}, u32[]{:S(2)}) collective-permute-start(bf16[128,2048]{1,0:T(8,128)(2,1)S(1)} %get-tuple-element.157), channel_id=1, source_target_pairs={{0,3},{1,2},{2,1},{3,0},{4,7},{5,6},{6,5},{7,4},{8,11},{9,10},{10,... | collective-permute-start | bytes 1572872 | tf_op jit(solution)/shard_map/ppermute | solution.py:52
  556.2 23.9 %collective-permute-start.50 = (bf16[128,2048]{1,0:T(8,128)(2,1)S(1)}, bf16[128,2048]{1,0:T(8,128)(2,1)S(1)}, u32[]{:S(2)}, u32[]{:S(2)}) collective-permute-start(bf16[128,2048]{1,0:T(8,128)(2,1)S(1)} %get-tuple-element.155), channel_id=1, source_target_pairs={{0,1},{1,0},{2,3},{3,2},{4,5},{5,4},{6,7},{7,6},{8,9},{9,8},{10,11... | collective-permute-start | bytes 1572872 | tf_op jit(solution)/shard_map/ppermute | solution.py:52
  557.8 36.4 %collective-permute-start.53 = (bf16[784,512]{1,0:T(8,128)(2,1)S(1)}, bf16[784,512]{1,0:T(8,128)(2,1)S(1)}, u32[]{:S(2)}, u32[]{:S(2)}) collective-permute-start(bf16[784,512]{1,0:T(8,128)(2,1)S(1)} %pad_maximum_fusion.15), channel_id=1, source_target_pairs={{0,4},{1,5},{2,6},{3,7},{4,8},{5,9},{6,10},{7,11},{8,12},{9,13},{1... | collective-permute-start | bytes 2408456 | tf_op jit(solution)/shard_map/ppermute | solution.py:52
  557.9 55.8 %collective-permute-start.54 = (bf16[784,512]{1,0:T(8,128)(2,1)S(1)}, bf16[784,512]{1,0:T(8,128)(2,1)}, u32[]{:S(2)}, u32[]{:S(2)}) collective-permute-start(bf16[784,512]{1,0:T(8,128)(2,1)S(1)} %pad_maximum_fusion.16), channel_id=1, source_target_pairs={{0,8},{1,9},{2,10},{3,11},{4,12},{5,13},{6,14},{7,15},{8,0},{9,1},... | collective-permute-start | bytes 2408456 | tf_op jit(solution)/shard_map/ppermute | solution.py:52
  580.6 36.8 %collective-permute-start.55 = (bf16[784,512]{1,0:T(8,128)(2,1)}, bf16[784,512]{1,0:T(8,128)(2,1)}, u32[]{:S(2)}, u32[]{:S(2)}) collective-permute-start(bf16[784,512]{1,0:T(8,128)(2,1)} %pad_maximum_fusion.17), channel_id=1, source_target_pairs={{0,12},{1,13},{2,14},{3,15},{4,0},{5,1},{6,2},{7,3},{8,4},{9,5},{1... | collective-permute-start | bytes 2408456 | tf_op jit(solution)/shard_map/ppermute | solution.py:52
  584.8 31.2 %collective-permute-start.67 = (bf16[4,64,1024]{2,1,0:T(8,128)(2,1)}, bf16[4,64,1024]{2,1,0:T(8,128)(2,1)}, u32[]{:S(2)}, u32[]{:S(2)}) collective-permute-start(bf16[4,64,1024]{2,1,0:T(8,128)(2,1)} %dynamic-slice_bitcast_fusion.4), channel_id=1, source_target_pairs={{0,16},{16,0},{1,17},{17,1},{2,18},{18,2},{3,19},{19,3},{4,20},{20... | collective-permute-start | bytes 1572872 | tf_op jit(solution)/shard_map/ppermute | solution.py:52
  588.7 33.1 %collective-permute-start.57 = (bf16[256,2048]{1,0:T(8,128)(2,1)}, bf16[256,2048]{1,0:T(8,128)(2,1)}, u32[]{:S(2)}, u32[]{:S(2)}) collective-permute-start(bf16[256,2048]{1,0:T(8,128)(2,1)} %get-tuple-element.249), channel_id=1, source_target_pairs={{0,2},{1,3},{2,0},{3,1},{4,6},{5,7},{6,4},{7,5},{8,10},{9,11},{10,... | collective-permute-start | bytes 3145736 | tf_op jit(solution)/shard_map/ppermute | solution.py:52
  594.2 27.6 %collective-permute-start.56 = (bf16[256,2048]{1,0:T(8,128)(2,1)}, bf16[256,2048]{1,0:T(8,128)(2,1)}, u32[]{:S(2)}, u32[]{:S(2)}) collective-permute-start(bf16[256,2048]{1,0:T(8,128)(2,1)} %get-tuple-element.250), channel_id=1, source_target_pairs={{0,1},{1,0},{2,3},{3,2},{4,5},{5,4},{6,7},{7,6},{8,9},{9,8},{10,11... | collective-permute-start | bytes 3145736 | tf_op jit(solution)/shard_map/ppermute | solution.py:52
  614.5 63.0 %collective-permute-start.66 = (bf16[256,2048]{1,0:T(8,128)(2,1)}, bf16[256,2048]{1,0:T(8,128)(2,1)}, u32[]{:S(2)}, u32[]{:S(2)}) collective-permute-start(bf16[256,2048]{1,0:T(8,128)(2,1)} %get-tuple-element.172), channel_id=1, source_target_pairs={{0,3},{1,2},{2,1},{3,0},{4,7},{5,6},{6,5},{7,4},{8,11},{9,10},{10,... | collective-permute-start | bytes 3145736 | tf_op jit(solution)/shard_map/ppermute | solution.py:52
  622.8 23.1 %collective-permute-start.60 = (bf16[2,64,1024]{2,1,0:T(8,128)(2,1)}, bf16[2,64,1024]{2,1,0:T(8,128)(2,1)S(1)}, u32[]{:S(2)}, u32[]{:S(2)}) collective-permute-start(bf16[2,64,1024]{2,1,0:T(8,128)(2,1)} %get-tuple-element.313), channel_id=1, source_target_pairs={{0,4},{1,5},{2,6},{3,7},{4,8},{5,9},{6,10},{7,11},{8,12},{9,13},{1... | collective-permute-start | bytes 786440 | tf_op jit(solution)/shard_map/ppermute | solution.py:52
  638.9 22.2 %collective-permute-start.58 = (bf16[2,64,1024]{2,1,0:T(8,128)(2,1)}, bf16[2,64,1024]{2,1,0:T(8,128)(2,1)S(1)}, u32[]{:S(2)}, u32[]{:S(2)}) collective-permute-start(bf16[2,64,1024]{2,1,0:T(8,128)(2,1)} %get-tuple-element.315), channel_id=1, source_target_pairs={{0,12},{1,13},{2,14},{3,15},{4,0},{5,1},{6,2},{7,3},{8,4},{9,5},{1... | collective-permute-start | bytes 786440 | tf_op jit(solution)/shard_map/ppermute | solution.py:52
  643.1 26.8 %collective-permute-start.65 = (bf16[64,2048]{1,0:T(8,128)(2,1)}, bf16[64,2048]{1,0:T(8,128)(2,1)S(1)}, u32[]{:S(2)}, u32[]{:S(2)}) collective-permute-start(bf16[64,2048]{1,0:T(8,128)(2,1)} %convert_element_type.524), channel_id=1, source_target_pairs={{0,0},{1,4},{2,8},{3,12},{4,1},{5,5},{6,9},{7,13},{8,2},{9,6},{10,... | collective-permute-start | bytes 786440 | tf_op jit(solution)/shard_map/ppermute | solution.py:52
  669.9 31.6 %collective-permute-start.68 = (bf16[4,64,1024]{2,1,0:T(8,128)(2,1)}, bf16[4,64,1024]{2,1,0:T(8,128)(2,1)}, u32[]{:S(2)}, u32[]{:S(2)}) collective-permute-start(bf16[4,64,1024]{2,1,0:T(8,128)(2,1)} %dynamic-slice_bitcast_fusion.3), channel_id=1, source_target_pairs={{0,16},{16,0},{1,17},{17,1},{2,18},{18,2},{3,19},{19,3},{4,20},{20... | collective-permute-start | bytes 1572872 | tf_op jit(solution)/shard_map/ppermute | solution.py:52
  (169 other events, 1581.0 us)
Sparse Core Ops, SparseCore 0:
  64.8 64.3 all-gather.4
  131.6 95.6 all-gather.6
